TPU v7x, 512 devices: a whole 4x4x16 slice. The times are simulated.
512 devices in a mesh: block: 64 (over z, y_lo, core), day: 8 (over x, y_hi).
Axes of the slice: x: 4, y: 4 (y_hi: 2, y_lo: 2; y = y_hi * 2 + y_lo), z: 16, core: 2. Of those that a mesh axis runs over, the one named last changes fastest.
Arguments:
- traces: float32 [8, 4096, 2400], P('day', 'block'), may hold values from -6 to 6
- counts: int32 [64], replicated, may hold values from 1 to 64, 3072 in all
- order: int32 [64], replicated, may hold values from 0 to 63, each once
Outputs:
- stacks: float32 [3, 64, 61, 4096], P(None, 'day', None, 'block')
Inputs may be any that keep to these rules, and one draw needn't show every extreme that they name: Slots from counts[b] to 63 of block b hold no channel; some block holds exactly 64. `order`: a permutation of the blocks; the window takes its first 3 entries as owners.
All inputs are finite; a program needn't handle non-finite values.
Results may differ from a plain program's by a relative error of at most 0.0037.
Values may be sent and summed in bfloat16 or wider, within the bound.
A program may use at most 128 MiB of HBM per device.

v0:
```python
import jax
import jax.numpy as jnp
from jax import lax
from jax.sharding import PartitionSpec as P

SEG = 2400
LAGS = 61
STEPS = 3
HALF = 30


clip_level = 2.5


def broadcast(value, axis, source):
    kept = jnp.where(lax.axis_index(axis) == source, value, 0).astype(value.dtype)
    return lax.psum(kept, axis)


def every_lag(padded, own_three):
    seg_len = own_three.shape[2]
    sums = []
    for lag in range(LAGS):
        window = padded[:, :, lag : lag + seg_len]
        sums.append(
            jnp.einsum("jsu,csu->jc", window, own_three, preferred_element_type=jnp.float32)
        )
    return jnp.stack(sums, 1)


def lag_sums(own_rows, owner_rows):
    capacity, samples = own_rows.shape
    owner_count = owner_rows.shape[0]
    segments = samples // SEG
    padded = jnp.pad(owner_rows.reshape(owner_count, segments, SEG), ((0, 0), (0, 0), (HALF, HALF)))
    own_three = own_rows.reshape(capacity, segments, SEG)
    return every_lag(padded, own_three)


def per_device(traces, counts, order):
    capacity = traces.shape[1]
    samples = traces.shape[2]
    block_index = lax.axis_index("block")
    live_count = lax.dynamic_index_in_dim(counts, block_index, 0, keepdims=False)
    pieces = traces[0].reshape(capacity, samples // SEG, SEG)
    centered = pieces - jnp.mean(pieces, axis=2, keepdims=True)
    rms = jnp.sqrt(jnp.mean(centered * centered, axis=2, keepdims=True) + 1e-05)
    slot = jnp.arange(capacity, dtype=jnp.int32)
    live = (slot < live_count).astype(jnp.float32)
    white = jnp.clip(centered / rms, -clip_level, clip_level) * live[:, None, None]
    own_rows = white.astype(jnp.bfloat16).reshape(capacity, samples)
    day_count = lax.axis_size("day")
    scale = float(day_count * samples) ** (-0.5)
    results = []
    for step in range(STEPS):
        owner_rows = broadcast(own_rows, "block", order[step])
        partial_value = lag_sums(own_rows, owner_rows)
        results.append(lax.psum_scatter(partial_value, "day", scatter_dimension=0, tiled=True))
    stacked = jnp.stack(results, 0)
    return stacked * scale


def solution(mesh):
    in_specs = (P("day", "block", None), P(), P())
    out_specs = P(None, "day", None, "block")
    return jax.shard_map(
        per_device, mesh=mesh, in_specs=in_specs, out_specs=out_specs, check_vma=False
    )
```

profile of v0, /device:TPU:6, one launch (start us, length us, event | category | flops | bytes accessed | tf_op | source)
XLA Modules:
  0.0 758.5 jit_solution(11040752436789546314)
XLA Ops:
  6.5 1.2 dynamic_slice.4
  8.4 1.2 reduce_sum.18
  9.7 1.4 fusion.187
  11.1 1.4 fusion.914
  14.4 2.0 broadcast_select_fusion.2
  17.6 435.0 %all-reduce.6.cloned.1.call-done = (bf16[64,2400]{1,0:T(8,128)(2,1)}, bf16[64,2400]{1,0:T(8,128)(2,1)}, bf16[64,2400]{1,0:T(8,128)(2,1)}) async-done(((bf16[64,2400]{1,0:T(8,128)(2,1)}, bf16[64,2400]{1,0:T(8,128)(2,1)}, bf16[64,2400]{1,0:T(8,128)(2,1)}), (bf16[64,2400]{1,0:T(8,128)(2,1)}, bf16[64,2400]{1,0:T(8,128)(2,1)}, bf16[64,2400]{1,0:T(8,128)(2,1)})) %all-reduce.6.cloned.1.call-update) | async-done | bytes 921616 | tf_op jit(solution)/shard_map/psum | solution.py:17
  452.6 1.3 fusion.121
  453.9 1.3 fusion.120
  455.2 1.3 fusion.119
  474.0 1.3 copy-done.4
  493.9 1.2 fusion.182
  496.9 0.9 fusion.179
  497.8 0.9 fusion.178
  498.7 0.9 fusion.177
  499.6 1.1 fusion.176
  503.4 0.9 fusion.172
  505.2 0.9 fusion.170
  506.1 0.9 fusion.169
  507.0 0.9 fusion.168
  507.9 0.9 fusion.167
  508.8 0.9 fusion.166
  510.6 0.9 fusion.164
  512.4 0.9 fusion.162
  514.2 0.9 fusion.160
  516.0 0.9 fusion.158
  517.8 0.9 fusion.156
  519.6 0.9 fusion.154
  523.2 0.9 fusion.150
  526.8 0.9 fusion.146
  528.6 0.9 fusion.144
  531.3 0.9 fusion.141
  532.2 0.9 fusion.140
  533.1 0.9 fusion.139
  534.0 0.9 fusion.138
  535.8 0.9 fusion.136
  536.7 0.9 fusion.135
  537.6 0.9 fusion.134
  538.5 0.9 fusion.133
  539.4 0.9 fusion.132
  541.3 0.9 fusion.130
  543.1 0.9 fusion.128
  544.0 0.9 fusion.127
  544.9 0.9 fusion.126
  548.5 0.9 fusion.122
  549.4 14.9 %reduce-scatter.6.cloned.1.call-done = f32[8,61,64]{2,0,1:T(8,128)} async-done(((f32[64,61,64]{2,0,1:T(8,128)}), f32[8,61,64]{2,0,1:T(8,128)}) %reduce-scatter.6.cloned.1.call-update) | async-done | bytes 124944 | tf_op jit(solution)/shard_map/reduce_scatter | solution.py:58
  564.3 92.8 %reduce-scatter.8.cloned.1.call-done = f32[8,61,64]{2,0,1:T(8,128)} async-done(((f32[64,61,64]{2,0,1:T(8,128)}), f32[8,61,64]{2,0,1:T(8,128)}) %reduce-scatter.8.cloned.1.call-update) | async-done | bytes 124944 | tf_op jit(solution)/shard_map/reduce_scatter | solution.py:58
  657.1 92.8 %reduce-scatter.4.cloned.1.call-done = f32[8,61,64]{2,0,1:T(8,128)} async-done(((f32[64,61,64]{2,0,1:T(8,128)}), f32[8,61,64]{2,0,1:T(8,128)}) %reduce-scatter.4.cloned.1.call-update) | async-done | bytes 124944 | tf_op jit(solution)/shard_map/reduce_scatter | solution.py:58
  749.9 2.1 maximum_multiply_fusion
  (170 shorter events, 61.3 us)
Async XLA Ops:
  6.5 446.1 %all-reduce.6.cloned.1.call-start = ((), (), s32[]{:S(2)}) async-start(), calls=%async_computation.6 | async-start | bytes 1867776 | tf_op jit(solution)/shard_map/psum | solution.py:17
  9.6 7.7 %copy-start.3 = (f32[1,64,2400]{2,1,0:T(8,128)S(1)}, f32[1,64,2400]{2,1,0:T(8,128)}, u32[]{:S(2)}) copy-start(f32[1,64,2400]{2,1,0:T(8,128)} %param.3) | copy-start | bytes 1843204
  17.3 547.0 %reduce-scatter.6.cloned.1.call-start = ((), (), s32[]{:S(2)}) async-start(), calls=%async_computation.4 | async-start | bytes 2248704 | tf_op jit(solution)/shard_map/reduce_scatter | solution.py:58
  452.6 3.9 copy-start.2
  473.0 2.5 copy-start.1
  473.9 1.3 copy-start.4
  475.3 181.8 %reduce-scatter.8.cloned.1.call-start = ((), (), s32[]{:S(2)}) async-start(), calls=%async_computation.5 | async-start | bytes 2248704 | tf_op jit(solution)/shard_map/reduce_scatter | solution.py:58
  492.1 1.8 copy-start
  493.9 6.8 copy-start.5
  541.2 208.7 %reduce-scatter.4.cloned.1.call-start = ((), (), s32[]{:S(2)}) async-start(), calls=%async_computation.3 | async-start | bytes 2248704 | tf_op jit(solution)/shard_map/reduce_scatter | solution.py:58
Sparse Core Ops, SparseCore 0:
  17.4 435.1 all-reduce.5
  475.4 88.8 reduce-scatter.5
  569.7 87.3 reduce-scatter.7
  662.3 87.4 reduce-scatter.3
where the time goes:
time: 759 us
  waiting for transfers between devices  636 us (84%)
  matrix products  94.2 us (12%)
  between operations  16 us (2%)
  other arithmetic  8.43 us (1%)
    psum x1, waiting for transfers between devices, broadcast(): return lax.psum(kept, axis)  435 us
    reduce_scatter x3, waiting for transfers between devices, per_device(): lax.psum_scatter(partial_value, 'day', scatter_dimension=0, tiled=True)  200 us
    dot_general x183, matrix products, every_lag(): jnp.einsum('jsu,csu->jc', window, own_three, preferred_element_type=jnp.f...  94.2 us
  transfers between devices with their start and end apart: 4, of which 4 were waited for; matrix products, arithmetic and copies ran while one was open for 10% of the time, Pallas kernels for 0%

commit v1 on v0

v1 whole, which is shorter than its diff:
```python
import jax
import jax.numpy as jnp
from jax import lax
from jax.experimental import pallas as pl
from jax.experimental.pallas import tpu as pltpu
from jax.sharding import PartitionSpec as P

MESH = pl.DeviceIdType.MESH

SEG = 2400
LAGS = 61
STEPS = 3
HALF = 30
CAP = 64
CLIP = 2.5
DAYS = 8
NZ = 16
PLANE = 4
SHARE = 8
FOLD = 10
WIDE = 2 * FOLD * 128
K = 2432
OWN_SHIFTS = 8
OWNER_SHIFTS = 8
ROWS = OWNER_SHIFTS * STEPS * SHARE
COLS = OWN_SHIFTS * CAP
PARTS = 15
PER = 4
F32 = jnp.float32
BF16 = jnp.bfloat16


def unfold(tiles):
    top, low = [], []
    for i in range(FOLD):
        tile = tiles[i].astype(F32)
        top.append(tile[0:8])
        low.append(tile[8:16])
    return jnp.concatenate(top + low, axis=1)[:, :K]


def kernel(order, counts, x_ref, out_ref, wide, gathered, first, chosen, along, full, shifted, acc,
           first_s, first_r, own_s, own_r, spread_s, spread_r, part_s, part_r, plane_s, plane_r):
    b = lax.axis_index("block")
    d = lax.axis_index("day")
    z = b // PLANE
    p = b % PLANE
    here = p * DAYS + d

    barrier = pltpu.get_barrier_semaphore()

    def greet_plane(k, _):
        m = (here + k) % (PLANE * DAYS)
        pl.semaphore_signal(barrier, 1, device_id=(z * PLANE + m // DAYS, m % DAYS), device_id_type=MESH)
        return 0

    def greet_line(k, _):
        pl.semaphore_signal(barrier, 1, device_id=(((z + k) % NZ) * PLANE + p, d), device_id_type=MESH)
        return 0

    lax.fori_loop(1, NZ, greet_line, 0)
    lax.fori_loop(1, PLANE * DAYS, greet_plane, 0)

    x = x_ref[0]
    centered = x - jnp.sum(x, axis=1, keepdims=True) * (1.0 / SEG)
    rms = jnp.sqrt(jnp.sum(centered * centered, axis=1, keepdims=True) * (1.0 / SEG) + 1e-05)
    live = (lax.broadcasted_iota(jnp.int32, (CAP, 1), 0) < counts[b]).astype(F32)
    wide[:, K - 128:] = jnp.zeros((CAP, WIDE - K + 128), F32)
    wide[:, :SEG] = jnp.clip(centered * (1.0 / rms), -CLIP, CLIP) * live
    for g in range(DAYS):
        for i in range(FOLD):
            top = wide[8 * g:8 * g + 8, 128 * i:128 * i + 128]
            low = wide[8 * g:8 * g + 8, 128 * (i + FOLD):128 * (i + FOLD) + 128]
            gathered[d, g, i] = jnp.concatenate([top, low], axis=0).astype(BF16)

    pl.semaphore_wait(barrier, NZ - 1 + PLANE * DAYS - 1)

    to_p = d // 2
    slot = p * 2 + d % 2

    def first_copy(k):
        to_d = (d + k) % DAYS
        return pltpu.make_async_remote_copy(
            gathered.at[d, to_d], first.at[slot], first_s.at[k], first_r.at[slot],
            device_id=(z * PLANE + to_p, to_d), device_id_type=MESH)

    for k in range(DAYS):
        if k == 0:
            @pl.when(p != to_p)
            def _():
                first_copy(0).start()

            @pl.when(p == to_p)
            def _():
                first[slot] = gathered[d, d]
        else:
            first_copy(k).start()

    def own_copy(k):
        return pltpu.make_async_remote_copy(
            gathered.at[d], gathered.at[d], own_s.at[k], own_r.at[d],
            device_id=(b, (d + k) % DAYS), device_id_type=MESH)

    def own_arrival(day):
        return pltpu.make_async_remote_copy(
            gathered.at[day], gathered.at[day], own_s.at[0], own_r.at[day],
            device_id=(b, day), device_id_type=MESH)

    for j in range(2 * PLANE):
        @pl.when(jnp.logical_or(p != to_p, slot != j))
        def _():
            pltpu.make_async_remote_copy(
                first.at[j], first.at[j], first_s.at[0], first_r.at[j],
                device_id=(b, d), device_id_type=MESH).wait_recv()

    for s in range(STEPS):
        for half in range(2):
            at = (s * 2 + half) * FOLD
            chosen[at:at + FOLD] = first[(order[s] % PLANE) * 2 + half]

    def spread_copy(k):
        to_z = (z + k) % NZ
        return to_z, pltpu.make_async_remote_copy(
            chosen.at[pl.ds(jnp.minimum(to_z, PARTS - 1) * PER, PER)], along.at[z], spread_s.at[k], spread_r.at[z],
            device_id=(to_z * PLANE + p, d), device_id_type=MESH)

    order_of_hops = [8, 7, 9, 6, 10, 5, 11, 4, 12, 3, 13, 2, 14, 1, 15]
    for k in order_of_hops:
        to_z, copy = spread_copy(k)

        @pl.when(to_z < PARTS)
        def _():
            copy.start()
    for k in range(1, DAYS):
        own_copy(k).start()

    def shifts_of_day(day):
        def group(g, _):
            rows = jnp.concatenate([unfold(gathered[day, 2 * g]), unfold(gathered[day, 2 * g + 1])], axis=0)
            for r in range(OWN_SHIFTS):
                rolled = rows if r == 0 else pltpu.roll(rows, r, 1)
                at = pl.multiple_of(r * CAP + g * 16, 16)
                shifted[day, pl.ds(at, 16), :] = rolled.astype(BF16)
            return 0
        lax.fori_loop(0, CAP // 16, group, 0)

    shifts_of_day(d)

    @pl.when(z < PARTS)
    def _():
        along[z] = chosen[pl.ds(z * PER, PER)]
        for k in range(1, NZ):
            src = (z + k) % NZ
            pltpu.make_async_remote_copy(
                along.at[src], along.at[src], spread_s.at[0], spread_r.at[src],
                device_id=(b, d), device_id_type=MESH).wait_recv()
        full[p, pl.ds(z * PER, PER)] = along[order[z // (PARTS // STEPS)] // PLANE]

    def part_copy(k):
        at = pl.ds(jnp.minimum(z, PARTS - 1) * PER, PER)
        return pltpu.make_async_remote_copy(
            full.at[p, at], full.at[p, at], part_s.at[k], part_r.at[jnp.minimum(z, PARTS - 1)],
            device_id=(((z + k) % NZ) * PLANE + p, d), device_id_type=MESH)

    @pl.when(z < PARTS)
    def _():
        for k in order_of_hops:
            part_copy(k).start()

    def more_days(k, _):
        day = (d + k) % DAYS
        own_arrival(day).wait_recv()
        shifts_of_day(day)
        return 0

    lax.fori_loop(1, 4, more_days, 0)

    for src in range(PARTS):
        @pl.when(src != z)
        def _():
            at = pl.ds(src * PER, PER)
            pltpu.make_async_remote_copy(
                full.at[p, at], full.at[p, at], part_s.at[0], part_r.at[src],
                device_id=(b, d), device_id_type=MESH).wait_recv()

    def plane_copy(k):
        return pltpu.make_async_remote_copy(
            full.at[p], full.at[p], plane_s.at[k], plane_r.at[p],
            device_id=(z * PLANE + (p + k) % PLANE, d), device_id_type=MESH)

    for k in (2, 1, 3):
        plane_copy(k).start()

    lax.fori_loop(4, DAYS, more_days, 0)

    acc[...] = jnp.zeros_like(acc)

    def day_sums(day):
        source, half = day // 2, day % 2
        rows = jnp.concatenate(
            [unfold(full[source, pl.ds(s * 2 * FOLD + half * FOLD, FOLD)]) for s in range(STEPS)], axis=0)
        left = jnp.concatenate(
            [pltpu.roll(rows, (HALF - OWN_SHIFTS * q) % K, 1) for q in range(OWNER_SHIFTS)], axis=0).astype(BF16)
        acc[...] += lax.dot_general(left, shifted[day], (((1,), (1,)), ((), ())), preferred_element_type=F32)

    def two_days(k, _):
        source = (p + k) % PLANE

        @pl.when(k > 0)
        def _():
            pltpu.make_async_remote_copy(
                full.at[source], full.at[source], plane_s.at[0], plane_r.at[source],
                device_id=(b, d), device_id_type=MESH).wait_recv()

        def one(half, _):
            day_sums(source * 2 + half)
            return 0
        lax.fori_loop(0, 2, one, 0)
        return 0

    lax.fori_loop(0, PLANE, two_days, 0)
    out_ref[...] = acc[...] * (float(DAYS * SEG) ** -0.5)

    @pl.when(p != to_p)
    def _():
        first_copy(0).wait_send()
    for k in range(1, DAYS):
        first_copy(k).wait_send()
        own_copy(k).wait_send()
    for k in order_of_hops:
        to_z, copy = spread_copy(k)

        @pl.when(to_z < PARTS)
        def _():
            copy.wait_send()

    @pl.when(z < PARTS)
    def _():
        for k in order_of_hops:
            part_copy(k).wait_send()
    for k in (2, 1, 3):
        plane_copy(k).wait_send()


def per_device(traces, counts, order):
    dma = pltpu.SemaphoreType.DMA
    tile = (16, 128)
    raw = pl.pallas_call(
        kernel,
        out_shape=jax.ShapeDtypeStruct((ROWS, COLS), F32),
        in_specs=[pl.BlockSpec(memory_space=pltpu.SMEM), pl.BlockSpec(memory_space=pltpu.SMEM),
                  pl.BlockSpec(memory_space=pltpu.VMEM)],
        out_specs=pl.BlockSpec(memory_space=pltpu.VMEM),
        scratch_shapes=[
            pltpu.VMEM((CAP, WIDE), F32),
            pltpu.VMEM((DAYS, DAYS, FOLD) + tile, BF16),
            pltpu.VMEM((2 * PLANE, FOLD) + tile, BF16),
            pltpu.VMEM((PARTS * PER,) + tile, BF16),
            pltpu.VMEM((NZ, PER) + tile, BF16),
            pltpu.VMEM((PLANE, PARTS * PER) + tile, BF16),
            pltpu.VMEM((DAYS, COLS, K), BF16),
            pltpu.VMEM((ROWS, COLS), F32),
            dma((DAYS,)), dma((2 * PLANE,)), dma((DAYS,)), dma((DAYS,)),
            dma((NZ,)), dma((NZ,)), dma((NZ,)), dma((NZ,)), dma((PLANE,)), dma((PLANE,)),
        ],
        compiler_params=pltpu.CompilerParams(
            collective_id=0, has_side_effects=True, vmem_limit_bytes=48 << 20),
        cost_estimate=pl.CostEstimate(flops=2 * ROWS * COLS * K * DAYS, bytes_accessed=1 << 20, transcendentals=0),
        name="correlate",
    )(order, counts, traces)
    parts = raw.reshape(OWNER_SHIFTS, STEPS, SHARE, OWN_SHIFTS, CAP)
    lags = parts.transpose(1, 2, 0, 3, 4).reshape(STEPS, SHARE, OWNER_SHIFTS * OWN_SHIFTS, CAP)
    return lags[:, :, :LAGS]


def solution(mesh):
    return jax.shard_map(
        per_device, mesh=mesh, in_specs=(P("day", "block", None), P(), P()),
        out_specs=P(None, "day", None, "block"), check_vma=False)
```

time: 759 us -> 88.4 us (0.12)
  the two profiles are of different devices: /device:TPU:6 before, /device:TPU:21 now
where the time goes in v1:
time: 88.4 us; the launch traced here: 88.2 us
  Pallas kernels  84.6 us (96%)
  local copies, waits for them, and re-layouts  3.61 us (4%)
    pallas_call x1, Pallas kernels, per_device(): pl.pallas_call(kernel, out_shape=jax.ShapeDtypeStruct((ROWS, COLS), F32),...  84.6 us
    unnamed x6, local copies, waits for them, and re-layouts  2.38 us

profile of v1, /device:TPU:21, one launch (start us, length us, event | category | flops | bytes accessed | tf_op | source)
XLA Modules:
  0.0 88.2 jit_solution(2828208436180798386)
XLA Ops:
  0.0 0.0 copy-start
  0.0 1.1 %copy-done = f32[1,64,2400]{2,1,0:T(8,128)S(1)} copy-done((f32[1,64,2400]{2,1,0:T(8,128)S(1)}, f32[1,64,2400]{2,1,0:T(8,128)}, u32[]{:S(2)}) %copy-start) | copy-done | bytes 614424
  1.1 0.0 copy-start.1
  1.1 0.7 copy-done.1
  1.7 0.0 copy-start.2
  1.7 0.7 copy-done.2
  2.4 84.6 %correlate.1 = f32[192,512]{1,0:T(8,128)S(1)} custom-call(s32[64]{0:T(128)S(1)} %copy-done.1, s32[64]{0:T(128)S(1)} %copy-done.2, f32[1,64,2400]{2,1,0:T(8,128)S(1)} %copy-done), custom_call_target="tpu_custom_call" | custom-call | flops 3825205248 | bytes 1048576 | tf_op jit(solution)/shard_map/correlate/pallas_call | solution.py:248
  87.0 0.2 reshape.6
  87.2 0.1 copy.4
  87.3 0.9 %slice.4 = f32[3,8,61,64]{3,1,2,0:T(8,128)} slice(f32[3,8,64,64]{3,1,2,0:T(8,128)S(1)} %bitcast.3), slice={[0:3], [0:8], [0:61], [0:64]} | slice | bytes 749568 | tf_op jit(solution)/shard_map/slice | solution.py:273
Async XLA Ops:
  0.0 1.1 %copy-start = (f32[1,64,2400]{2,1,0:T(8,128)S(1)}, f32[1,64,2400]{2,1,0:T(8,128)}, u32[]{:S(2)}) copy-start(f32[1,64,2400]{2,1,0:T(8,128)} %x_ref.1) | copy-start | bytes 1843204
  1.1 0.7 copy-start.1
  1.7 0.7 copy-start.2

commit v2 on v0

v2 whole, which is shorter than its diff:
```python
import jax
import jax.numpy as jnp
from jax import lax
from jax.experimental import pallas as pl
from jax.experimental.pallas import tpu as pltpu
from jax.sharding import PartitionSpec as P

MESH = pl.DeviceIdType.MESH

SEG = 2400
LAGS = 61
STEPS = 3
HALF = 30
CAP = 64
CLIP = 2.5
DAYS = 8
NZ = 16
NX = 4
PLANE = 4
TILES = 19
K = TILES * 128
SHARE = 16
OWN_SHIFTS = 8
OWNER_SHIFTS = 8
ROWS = OWNER_SHIFTS * STEPS * SHARE // 2
COLS = OWN_SHIFTS * CAP
CLASSES = 4
PER = 5
GROUP = STEPS * PER
F32 = jnp.float32
BF16 = jnp.bfloat16


def kernel(order_hbm, counts_hbm, x_hbm, out_ref, order, counts, x_ref, wide, gathered, first, far, full,
           shifted, acc, outgoing, incoming, load, first_s, first_r, own_s, own_r, far_s, far_r, full_r,
           line_s, core_s, sum_s, sum_r):
    b = lax.axis_index("block")
    d = lax.axis_index("day")
    z = b // PLANE
    p = b % PLANE
    x = d // 2
    yh = d % 2
    mine = z % CLASSES
    two = 2 - 4 * (p % 2)
    two_x = 2 - 4 * (x % 2)
    q = (p + 2) % PLANE
    mate = p + 1 - 2 * (p % 2)

    def at_device(hop, plane, day):
        return ((z + hop + NZ) % NZ) * PLANE + plane, day

    def day_at(k):
        return ((x + k) % NX) * 2 + yh

    loads = [pltpu.make_async_copy(x_hbm.at[0], x_ref, load.at[0]),
             pltpu.make_async_copy(order_hbm, order, load.at[1]),
             pltpu.make_async_copy(counts_hbm, counts, load.at[2])]
    for copy in loads:
        copy.start()

    barrier = pltpu.get_barrier_semaphore()

    def greet(device):
        pl.semaphore_signal(barrier, 1, device_id=device, device_id_type=MESH)

    spots = ((two, q), (two, p), (1, q), (-1, q), (1, p), (-1, p), (0, q))
    for j in (2, 1, 3):
        greet(at_device(CLASSES * j, p, d))
    for i, hop in enumerate((-two, -1, 1, 0)):
        for plane in range(PLANE):
            device = at_device(hop, plane, p * 2 + yh)
            if i < 3:
                greet(device)
            else:
                @pl.when(jnp.logical_or(plane != p, p != x))
                def _():
                    greet(device)
    for hop, plane in spots:
        greet(at_device(-hop, plane, d))
    for k in range(1, NX):
        greet(at_device(0, p, day_at(k)))
    greet(at_device(0, mate, d))
    greet(at_device(0, p, x * 2 + 1 - yh))
    for copy in loads:
        copy.wait()

    rows = x_ref[...]
    centered = rows - jnp.sum(rows, axis=1, keepdims=True) * (1.0 / SEG)
    rms = jnp.sqrt(jnp.sum(centered * centered, axis=1, keepdims=True) * (1.0 / SEG) + 1e-05)
    live = (lax.broadcasted_iota(jnp.int32, (CAP, 1), 0) < counts[b]).astype(F32)
    wide[:, K - 128:] = jnp.zeros((CAP, 128), F32)
    wide[:, :SEG] = jnp.clip(centered * (1.0 / rms), -CLIP, CLIP) * live
    for g in range(NX):
        for i in range(TILES):
            gathered[x, g, i] = wide[16 * g:16 * g + 16, 128 * i:128 * i + 128].astype(BF16)
        gathered[x, g, TILES] = jnp.zeros((16, 128), BF16)

    pl.semaphore_wait(barrier, 31 - (p == x).astype(jnp.int32))

    hops = (0, 1, -1, two_x)

    def first_copy(i, k):
        to_class = (z + hops[i] + NZ) % CLASSES
        return pltpu.make_async_remote_copy(
            gathered.at[x, (x + k) % NX, pl.ds(to_class * PER, PER)], first.at[i * PLANE + p],
            first_s.at[i * NX + k], first_r.at[i * PLANE + p],
            device_id=at_device(hops[i], x, day_at(k)), device_id_type=MESH)

    @pl.when(p != x)
    def _():
        first_copy(0, 0).start()

    @pl.when(p == x)
    def _():
        first[p] = gathered[x, x, pl.ds(mine * PER, PER)]

    firsts = [(i, k) for k in (2, 1, 3, 0) for i in (3, 1, 2, 0) if i or k]
    for i, k in firsts:
        first_copy(i, k).start()

    def own_copy(k):
        return pltpu.make_async_remote_copy(
            gathered.at[x], gathered.at[x], own_s.at[k], own_r.at[x],
            device_id=at_device(0, p, day_at(k)), device_id_type=MESH)

    def shifts_of_day(day):
        def group(g, _):
            rows = jnp.concatenate([gathered[day, g, i].astype(F32) for i in range(TILES)], axis=1)
            for r in range(OWN_SHIFTS):
                rolled = rows if r == 0 else pltpu.roll(rows, r, 1)
                at = pl.multiple_of(r * CAP + g * 16, 16)
                shifted[day, pl.ds(at, 16), :] = rolled.astype(BF16)
            return 0
        lax.fori_loop(0, CAP // 16, group, 0)

    def own_shifts(k, _):
        day = (x + NX - k) % NX
        pltpu.make_async_remote_copy(
            gathered.at[day], gathered.at[day], own_s.at[k], own_r.at[day],
            device_id=(b, d), device_id_type=MESH).wait_recv()
        shifts_of_day(day)
        return 0

    shifts_of_day(x)
    for j in range(CLASSES * PLANE):
        @pl.when(jnp.logical_or(p != x, p != j))
        def _():
            pltpu.make_async_remote_copy(
                first.at[j], first.at[j], first_s.at[0], first_r.at[j],
                device_id=(b, d), device_id_type=MESH).wait_recv()

    for s in range(STEPS):
        gap = (z - order[s] // PLANE + NZ) % NZ
        came = jnp.where(gap == 1, 1, jnp.where(gap == NZ - 1, 2, jnp.where(gap == (two + NZ) % NZ, 3, 0)))
        far[z // CLASSES, s * PER:(s + 1) * PER] = first[came * PLANE + order[s] % PLANE]

    def far_copy(j):
        return pltpu.make_async_remote_copy(
            far.at[z // CLASSES], far.at[z // CLASSES], far_s.at[j], far_r.at[z // CLASSES],
            device_id=at_device(CLASSES * j, p, d), device_id_type=MESH)

    for j in (2, 1, 3):
        far_copy(j).start()
    for k in (1, 3, 2):
        own_copy(k).start()
    for j in (1, 3, 2):
        src = (z // CLASSES + j) % CLASSES
        pltpu.make_async_remote_copy(
            far.at[src], far.at[src], far_s.at[j], far_r.at[src],
            device_id=(b, d), device_id_type=MESH).wait_recv()
    for s in range(STEPS):
        owner_z = order[s] // PLANE
        gap = (mine - owner_z + NZ) % CLASSES
        step = jnp.where(gap == 3, -1, jnp.where(gap == 2, two, gap))
        sender = (owner_z + step + NZ) % NZ
        full[p, mine, s * PER:(s + 1) * PER] = far[sender // CLASSES, s * PER:(s + 1) * PER]

    def piece(part, cls, sem, to):
        return pltpu.make_async_remote_copy(
            full.at[part, cls], full.at[part, cls], sem, full_r.at[part, cls],
            device_id=to, device_id_type=MESH)

    core = at_device(0, mate, d)

    def spread(j):
        hop, plane = spots[j]
        return piece(p, mine, line_s.at[j], at_device(hop, plane, d))

    def arrival(part, cls):
        piece(part, cls, line_s.at[0], (b, d)).wait_recv()

    def to_core(part, cls):
        piece(part, cls, core_s.at[part, cls], core).start()

    for j in range(len(spots)):
        spread(j).start()
    to_core(p, mine)

    lax.fori_loop(1, NX, own_shifts, 0)

    others = [(z + k + NZ) % CLASSES for k in (1, 3, 2)]
    arrival(q, mine)
    to_core(q, mine)
    for cls in others:
        arrival(p, cls)
        to_core(p, cls)
    for cls in others:
        arrival(q, cls)
        to_core(q, cls)

    acc[...] = jnp.zeros_like(acc)

    def owner_rows(day):
        theirs, ours = [], []
        for s in range(STEPS):
            top, low = [], []
            for t in range(TILES):
                tile = full[day, t // PER, s * PER + t % PER].astype(F32)
                top.append(tile[0:8])
                low.append(tile[8:16])
            top = jnp.concatenate(top, axis=1)
            low = jnp.concatenate(low, axis=1)
            theirs.append(jnp.where(yh == 0, low, top))
            ours.append(jnp.where(yh == 0, top, low))
        return jnp.concatenate(theirs, axis=0), jnp.concatenate(ours, axis=0)

    def add_sums(half, day, rows):
        left = jnp.concatenate(
            [pltpu.roll(rows, (HALF - OWN_SHIFTS * n) % K, 1) for n in range(OWNER_SHIFTS)], axis=0).astype(BF16)
        acc[half] += lax.dot_general(left, shifted[day], (((1,), (1,)), ((), ())), preferred_element_type=F32)

    def whole_day(day):
        theirs, ours = owner_rows(day)
        add_sums(0, day, theirs)
        add_sums(1, day, ours)

    def two_days(k, _):
        whole_day((p + 2 * k) % PLANE)
        return 0

    lax.fori_loop(0, 2, two_days, 0)
    for cls in range(CLASSES):
        arrival(mate, cls)
    whole_day(mate)
    last = (mate + 2) % PLANE
    for cls in range(CLASSES):
        arrival(last, cls)
    theirs, ours = owner_rows(last)
    add_sums(0, last, theirs)
    outgoing[...] = acc[0].astype(BF16)

    def sum_copy():
        return pltpu.make_async_remote_copy(
            outgoing, incoming, sum_s, sum_r, device_id=at_device(0, p, x * 2 + 1 - yh), device_id_type=MESH)

    sum_copy().start()
    add_sums(1, last, ours)

    @pl.when(p != x)
    def _():
        first_copy(0, 0).wait_send()
    for i, k in firsts:
        first_copy(i, k).wait_send()
    for k in range(1, NX):
        own_copy(k).wait_send()
        far_copy(k).wait_send()
    for j in range(len(spots)):
        spread(j).wait_send()
    for part in (p, q):
        for cls in range(CLASSES):
            piece(part, cls, core_s.at[part, cls], core).wait_send()
    sum_copy().wait()
    out_ref[...] = (acc[1] + incoming[...].astype(F32)) * (float(DAYS * SEG) ** -0.5)


def per_device(traces, counts, order):
    dma = pltpu.SemaphoreType.DMA
    tile = (16, 128)
    raw = pl.pallas_call(
        kernel,
        out_shape=jax.ShapeDtypeStruct((ROWS, COLS), F32),
        in_specs=[pl.BlockSpec(memory_space=pltpu.HBM)] * 3,
        out_specs=pl.BlockSpec(memory_space=pltpu.VMEM),
        scratch_shapes=[
            pltpu.SMEM(order.shape, jnp.int32),
            pltpu.SMEM(counts.shape, jnp.int32),
            pltpu.VMEM((CAP, SEG), F32),
            pltpu.VMEM((CAP, K), F32),
            pltpu.VMEM((NX, NX, TILES + 1) + tile, BF16),
            pltpu.VMEM((CLASSES * PLANE, PER) + tile, BF16),
            pltpu.VMEM((CLASSES, GROUP) + tile, BF16),
            pltpu.VMEM((PLANE, CLASSES, GROUP) + tile, BF16),
            pltpu.VMEM((NX, COLS, K), BF16),
            pltpu.VMEM((2, ROWS, COLS), F32),
            pltpu.VMEM((ROWS, COLS), BF16),
            pltpu.VMEM((ROWS, COLS), BF16),
            dma((3,)), dma((CLASSES * NX,)), dma((CLASSES * PLANE,)), dma((NX,)), dma((NX,)),
            dma((CLASSES,)), dma((CLASSES,)), dma((PLANE, CLASSES)),
            dma((7,)), dma((PLANE, CLASSES)), dma, dma,
        ],
        compiler_params=pltpu.CompilerParams(
            collective_id=0, has_side_effects=True, vmem_limit_bytes=63 << 20),
        cost_estimate=pl.CostEstimate(flops=2 * ROWS * COLS * K * DAYS, bytes_accessed=1 << 20, transcendentals=0),
        name="correlate",
    )(order, counts, traces)
    parts = raw.reshape(OWNER_SHIFTS, STEPS, SHARE // 2, OWN_SHIFTS, CAP)
    lags = parts.transpose(1, 2, 0, 3, 4).reshape(STEPS, SHARE // 2, OWNER_SHIFTS * OWN_SHIFTS, CAP)
    return lags[:, :, :LAGS]


def solution(mesh):
    return jax.shard_map(
        per_device, mesh=mesh, in_specs=(P("day", "block", None), P(), P()),
        out_specs=P(None, "day", None, "block"), check_vma=False)
```

time: 759 us -> 61.1 us (0.08)
  the two profiles are of different devices: /device:TPU:6 before, /device:TPU:3 now
where the time goes in v2:
time: 61.1 us; the launch traced here: 61 us
  Pallas kernels  58.7 us (96%)
  local copies, waits for them, and re-layouts  2.22 us (4%)
    pallas_call x1, Pallas kernels, per_device(): pl.pallas_call(kernel, out_shape=jax.ShapeDtypeStruct((ROWS, COLS), F32),...  58.7 us

profile of v2, /device:TPU:3, one launch (start us, length us, event | category | flops | bytes accessed | tf_op | source)
XLA Modules:
  0.0 61.0 jit_solution(12315458928970693634)
XLA Ops:
  0.0 58.7 %correlate.1 = f32[192,512]{1,0:T(8,128)} custom-call(s32[64]{0:T(128)} %order_hbm.1, s32[64]{0:T(128)} %counts_hbm.1, f32[1,64,2400]{2,1,0:T(8,128)} %x_hbm.1), custom_call_target="tpu_custom_call" | custom-call | flops 3825205248 | bytes 1048576 | tf_op jit(solution)/shard_map/correlate/pallas_call | solution.py:279
  58.7 1.2 %reshape.6 = f32[8,3,8,8,64]{4,3,2,1,0:T(8,128)S(1)} reshape(f32[192,512]{1,0:T(8,128)} %correlate.1) | data formatting | bytes 786432 | tf_op jit(solution)/shard_map/reshape | solution.py:306
  59.9 0.1 copy.4
  60.0 0.9 %slice.4 = f32[3,8,61,64]{3,1,2,0:T(8,128)} slice(f32[3,8,64,64]{3,1,2,0:T(8,128)S(1)} %bitcast.3), slice={[0:3], [0:8], [0:61], [0:64]} | slice | bytes 749568 | tf_op jit(solution)/shard_map/slice | solution.py:308

commit v3 on v2

v3 whole, which is shorter than its diff:
```python
import jax
import jax.numpy as jnp
from jax import lax
from jax.experimental import pallas as pl
from jax.experimental.pallas import tpu as pltpu
from jax.sharding import PartitionSpec as P

MESH = pl.DeviceIdType.MESH

SEG = 2400
LAGS = 61
STEPS = 3
HALF = 30
CAP = 64
CLIP = 2.5
DAYS = 8
NZ = 16
NX = 4
PLANE = 4
TILES = 19
K = TILES * 128
SHARE = 16
OWN_SHIFTS = 4
OWNER_SHIFTS = 16
ROWS = OWNER_SHIFTS * SHARE // 2
COLS = OWN_SHIFTS * CAP
CLASSES = 4
PER = 5
F32 = jnp.float32
BF16 = jnp.bfloat16


def kernel(order_hbm, counts_hbm, x_hbm, out_ref, order, counts, x_ref, wide, gathered, first, far_0, far_1, far_2, full,
           shifted, acc, outgoing, incoming, load, first_s, first_r, own_s, own_r, far_s, far_r, full_r,
           line_s, core_s, core_r, sum_s, sum_r):
    far = (far_0, far_1, far_2)
    b = lax.axis_index("block")
    d = lax.axis_index("day")
    z = b // PLANE
    p = b % PLANE
    x = d // 2
    yh = d % 2
    mine = z % CLASSES
    two = 2 - 4 * (p % 2)
    two_x = 2 - 4 * (x % 2)
    q = (p + 2) % PLANE
    mate = p + 1 - 2 * (p % 2)

    def at_device(hop, plane, day):
        return ((z + hop + NZ) % NZ) * PLANE + plane, day

    def day_at(k):
        return ((x + k) % NX) * 2 + yh

    loads = [pltpu.make_async_copy(x_hbm.at[0], x_ref, load.at[0]),
             pltpu.make_async_copy(order_hbm, order, load.at[1]),
             pltpu.make_async_copy(counts_hbm, counts, load.at[2])]
    for copy in loads:
        copy.start()

    barrier = pltpu.get_barrier_semaphore()

    def greet(device):
        pl.semaphore_signal(barrier, 1, device_id=device, device_id_type=MESH)

    spots = ((two, q), (two, p), (1, q), (-1, q), (1, p), (-1, p), (0, q))
    for j in (2, 1, 3):
        greet(at_device(CLASSES * j, p, d))
    for i, hop in enumerate((-two, -1, 1, 0)):
        for plane in range(PLANE):
            device = at_device(hop, plane, p * 2 + yh)
            if i < 3:
                greet(device)
            else:
                @pl.when(jnp.logical_or(plane != p, p != x))
                def _():
                    greet(device)
    for hop, plane in spots:
        greet(at_device(-hop, plane, d))
    for k in range(1, NX):
        greet(at_device(0, p, day_at(k)))
    greet(at_device(0, mate, d))
    greet(at_device(0, p, x * 2 + 1 - yh))
    for copy in loads:
        copy.wait()

    rows = x_ref[...]
    centered = rows - jnp.sum(rows, axis=1, keepdims=True) * (1.0 / SEG)
    rms = jnp.sqrt(jnp.sum(centered * centered, axis=1, keepdims=True) * (1.0 / SEG) + 1e-05)
    live = (lax.broadcasted_iota(jnp.int32, (CAP, 1), 0) < counts[b]).astype(F32)
    wide[:, K - 128:] = jnp.zeros((CAP, 128), F32)
    wide[:, :SEG] = jnp.clip(centered * (1.0 / rms), -CLIP, CLIP) * live
    for g in range(NX):
        for i in range(TILES):
            gathered[x, g, i] = wide[16 * g:16 * g + 16, 128 * i:128 * i + 128].astype(BF16)
        gathered[x, g, TILES] = jnp.zeros((16, 128), BF16)

    pl.semaphore_wait(barrier, 31 - (p == x).astype(jnp.int32))

    hops = (0, 1, -1, two_x)

    def first_copy(i, k):
        to_class = (z + hops[i] + NZ) % CLASSES
        return pltpu.make_async_remote_copy(
            gathered.at[x, (x + k) % NX, pl.ds(to_class * PER, PER)], first.at[i * PLANE + p],
            first_s.at[i * NX + k], first_r.at[i * PLANE + p],
            device_id=at_device(hops[i], x, day_at(k)), device_id_type=MESH)

    @pl.when(p != x)
    def _():
        first_copy(0, 0).start()

    @pl.when(p == x)
    def _():
        first[p] = gathered[x, x, pl.ds(mine * PER, PER)]

    firsts = [(i, k) for k in (2, 1, 3, 0) for i in (3, 1, 2, 0) if i or k]
    for i, k in firsts:
        first_copy(i, k).start()

    def own_copy(k):
        return pltpu.make_async_remote_copy(
            gathered.at[x], gathered.at[x], own_s.at[k], own_r.at[x],
            device_id=at_device(0, p, day_at(k)), device_id_type=MESH)

    for k in (1, 3, 2):
        own_copy(k).start()

    def shifts_of_day(day):
        def group(g, _):
            rows = jnp.concatenate([gathered[day, g, i] for i in range(TILES)], axis=1)
            for r in range(OWN_SHIFTS):
                rolled = rows if r == 0 else pltpu.roll(rows, r, 1)
                at = pl.multiple_of(r * CAP + g * 16, 16)
                shifted[day, pl.ds(at, 16), :] = rolled
            return 0
        lax.fori_loop(0, CAP // 16, group, 0)

    def own_shifts(k, _):
        day = (x + NX - k) % NX
        pltpu.make_async_remote_copy(
            gathered.at[day], gathered.at[day], own_s.at[k], own_r.at[day],
            device_id=(b, d), device_id_type=MESH).wait_recv()
        shifts_of_day(day)
        return 0

    shifts_of_day(x)
    for j in range(CLASSES * PLANE):
        @pl.when(jnp.logical_or(p != x, p != j))
        def _():
            pltpu.make_async_remote_copy(
                first.at[j], first.at[j], first_s.at[0], first_r.at[j],
                device_id=(b, d), device_id_type=MESH).wait_recv()

    def far_copy(s, j):
        return pltpu.make_async_remote_copy(
            far[s].at[z // CLASSES], far[s].at[z // CLASSES], far_s.at[s, j], far_r.at[s, z // CLASSES],
            device_id=at_device(CLASSES * j, p, d), device_id_type=MESH)

    for s in range(STEPS):
        gap = (z - order[s] // PLANE + NZ) % NZ
        came = jnp.where(gap == 1, 1, jnp.where(gap == NZ - 1, 2, jnp.where(gap == (two + NZ) % NZ, 3, 0)))
        far[s][z // CLASSES] = first[came * PLANE + order[s] % PLANE]
        for j in (2, 1, 3):
            far_copy(s, j).start()

    def piece(s, part, cls, sem, to):
        return pltpu.make_async_remote_copy(
            full.at[s, part, cls], full.at[s, part, cls], sem, full_r.at[s * PLANE + part, cls],
            device_id=to, device_id_type=MESH)

    core = at_device(0, mate, d)

    def spread(s, j):
        hop, plane = spots[j]
        return piece(s, p, mine, line_s.at[s, j], at_device(hop, plane, d))

    def arrival(s, part, cls):
        piece(s, part, cls, line_s.at[0, 0], (b, d)).wait_recv()

    def core_copy(s, part):
        return pltpu.make_async_remote_copy(
            full.at[s, part], full.at[s, part], core_s.at[s, part], core_r.at[s, part],
            device_id=core, device_id_type=MESH)

    others = [(z + k + NZ) % CLASSES for k in (1, 3, 2)]

    def open_owner(s):
        for j in (1, 3, 2):
            src = (z // CLASSES + j) % CLASSES
            pltpu.make_async_remote_copy(
                far[s].at[src], far[s].at[src], far_s.at[s, j], far_r.at[s, src],
                device_id=(b, d), device_id_type=MESH).wait_recv()
        owner_z = order[s] // PLANE
        gap = (mine - owner_z + NZ) % CLASSES
        step = jnp.where(gap == 3, -1, jnp.where(gap == 2, two, gap))
        sender = (owner_z + step + NZ) % NZ
        full[s, p, mine] = far[s][sender // CLASSES]
        for j in range(len(spots)):
            spread(s, j).start()

    def pass_on(s):
        for cls in others:
            arrival(s, p, cls)
        core_copy(s, p).start()
        arrival(s, q, mine)
        for cls in others:
            arrival(s, q, cls)
        core_copy(s, q).start()

    def from_core(s):
        for part in (mate, (mate + 2) % PLANE):
            core_copy(s, part).wait_recv()

    def add_days(s, part):
        def one(k, _):
            day = (part + 2 * k) % PLANE
            rows = jnp.concatenate(
                [full[s, day, t // PER, t % PER] for t in range(TILES)], axis=1)
            left = jnp.concatenate(
                [pltpu.roll(rows, (HALF - OWN_SHIFTS * n) % K, 1) for n in range(OWNER_SHIFTS)], axis=0)
            sums = lax.dot_general(left, shifted[day], (((1,), (1,)), ((), ())), preferred_element_type=F32)
            acc[s] += sums
            return 0
        lax.fori_loop(0, 2, one, 0)

    def sum_copy(s):
        return pltpu.make_async_remote_copy(
            outgoing.at[s], incoming.at[s], sum_s.at[s], sum_r.at[s],
            device_id=at_device(0, p, x * 2 + 1 - yh), device_id_type=MESH)

    def halves(s):
        whole = acc[s].reshape(OWNER_SHIFTS, 2, SHARE // 2, COLS)
        return whole[:, 0].reshape(ROWS, COLS), whole[:, 1].reshape(ROWS, COLS)

    def to_partner(s):
        top, low = halves(s)
        outgoing[s] = jnp.where(yh == 0, low, top).astype(BF16)
        sum_copy(s).start()

    def finish(s):
        sum_copy(s).wait_recv()
        top, low = halves(s)
        out_ref[s] = (jnp.where(yh == 0, top, low) + incoming[s].astype(F32)) * (float(DAYS * SEG) ** -0.5)

    acc[...] = jnp.zeros_like(acc)
    open_owner(0)
    open_owner(1)
    own_shifts(1, 0)
    open_owner(2)
    lax.fori_loop(2, NX, own_shifts, 0)
    pass_on(0)
    add_days(0, p)
    pass_on(1)
    from_core(0)
    add_days(0, mate)
    to_partner(0)
    add_days(1, p)
    pass_on(2)
    from_core(1)
    add_days(1, mate)
    to_partner(1)
    add_days(2, p)
    from_core(2)
    add_days(2, mate)
    to_partner(2)

    @pl.when(p != x)
    def _():
        first_copy(0, 0).wait_send()
    for i, k in firsts:
        first_copy(i, k).wait_send()
    for k in range(1, NX):
        own_copy(k).wait_send()
    for s in range(STEPS):
        for k in range(1, NX):
            far_copy(s, k).wait_send()
        for j in range(len(spots)):
            spread(s, j).wait_send()
        for part in (p, q):
            core_copy(s, part).wait_send()
    for s in range(STEPS):
        finish(s)
        sum_copy(s).wait_send()


def per_device(traces, counts, order):
    dma = pltpu.SemaphoreType.DMA
    tile = (16, 128)
    raw = pl.pallas_call(
        kernel,
        out_shape=jax.ShapeDtypeStruct((STEPS, ROWS, COLS), F32),
        in_specs=[pl.BlockSpec(memory_space=pltpu.HBM)] * 3,
        out_specs=pl.BlockSpec(memory_space=pltpu.VMEM),
        scratch_shapes=[
            pltpu.SMEM(order.shape, jnp.int32),
            pltpu.SMEM(counts.shape, jnp.int32),
            pltpu.VMEM((CAP, SEG), F32),
            pltpu.VMEM((CAP, K), F32),
            pltpu.VMEM((NX, NX, TILES + 1) + tile, BF16),
            pltpu.VMEM((CLASSES * PLANE, PER) + tile, BF16),
            pltpu.VMEM((CLASSES, PER) + tile, BF16),
            pltpu.VMEM((CLASSES, PER) + tile, BF16),
            pltpu.VMEM((CLASSES, PER) + tile, BF16),
            pltpu.VMEM((STEPS, PLANE, CLASSES, PER) + tile, BF16),
            pltpu.VMEM((NX, COLS, K), BF16),
            pltpu.VMEM((STEPS, 2 * ROWS, COLS), F32),
            pltpu.VMEM((STEPS, ROWS, COLS), BF16),
            pltpu.VMEM((STEPS, ROWS, COLS), BF16),
            dma((3,)), dma((CLASSES * NX,)), dma((CLASSES * PLANE,)), dma((NX,)), dma((NX,)),
            dma((STEPS, CLASSES)), dma((STEPS, CLASSES)), dma((STEPS * PLANE, CLASSES)),
            dma((STEPS, 7)), dma((STEPS, PLANE)), dma((STEPS, PLANE)), dma((STEPS,)), dma((STEPS,)),
        ],
        compiler_params=pltpu.CompilerParams(
            collective_id=0, has_side_effects=True, vmem_limit_bytes=63 << 20),
        cost_estimate=pl.CostEstimate(flops=2 * STEPS * ROWS * COLS * K * DAYS, bytes_accessed=1 << 20, transcendentals=0),
        name="correlate",
    )(order, counts, traces)
    parts = raw.reshape(STEPS, OWNER_SHIFTS, SHARE // 2, OWN_SHIFTS, CAP)
    lags = parts.transpose(0, 2, 1, 3, 4).reshape(STEPS, SHARE // 2, OWNER_SHIFTS * OWN_SHIFTS, CAP)
    return lags[:, :, :LAGS]


def solution(mesh):
    return jax.shard_map(
        per_device, mesh=mesh, in_specs=(P("day", "block", None), P(), P()),
        out_specs=P(None, "day", None, "block"), check_vma=False)
```

time: 61.1 us -> 56.6 us (0.926)
  the two profiles are of different devices: /device:TPU:3 before, /device:TPU:1 now
where the time goes in v3:
time: 56.6 us; the launch traced here: 56.4 us
  Pallas kernels  54.1 us (96%)
  local copies, waits for them, and re-layouts  2.3 us (4%)
    pallas_call x1, Pallas kernels, per_device(): pl.pallas_call(kernel, out_shape=jax.ShapeDtypeStruct((STEPS, ROWS, COLS)...  54.1 us
    reshape x1, local copies, waits for them, and re-layouts, per_device(): parts = raw.reshape(STEPS, OWNER_SHIFTS, SHARE // 2, OWN_SHIFTS, CAP)  1.33 us

profile of v3, /device:TPU:1, one launch (start us, length us, event | category | flops | bytes accessed | tf_op | source)
XLA Modules:
  0.0 56.4 jit_solution(9622538208559514964)
XLA Ops:
  0.0 54.1 %correlate.1 = f32[3,128,256]{2,1,0:T(8,128)} custom-call(s32[64]{0:T(128)} %order_hbm.1, s32[64]{0:T(128)} %counts_hbm.1, f32[1,64,2400]{2,1,0:T(8,128)} %x_hbm.1), custom_call_target="tpu_custom_call" | custom-call | flops 3825205248 | bytes 1048576 | tf_op jit(solution)/shard_map/correlate/pallas_call | solution.py:290
  54.1 1.3 %reshape.6 = f32[3,16,8,4,64]{4,3,2,1,0:T(4,128)S(1)} reshape(f32[3,128,256]{2,1,0:T(8,128)} %correlate.1) | data formatting | bytes 786432 | tf_op jit(solution)/shard_map/reshape | solution.py:319
  55.4 0.1 copy.4
  55.5 0.9 %slice.4 = f32[3,8,61,64]{3,1,2,0:T(8,128)} slice(f32[3,8,64,64]{3,1,2,0:T(8,128)S(1)} %bitcast.3), slice={[0:3], [0:8], [0:61], [0:64]} | slice | bytes 749568 | tf_op jit(solution)/shard_map/slice | solution.py:321

commit v4 on v3

--- a/solution.py
+++ b/solution.py
@@ -30,9 +30,9 @@
 BF16 = jnp.bfloat16
 
 
-def kernel(order_hbm, counts_hbm, x_hbm, out_ref, order, counts, x_ref, wide, gathered, first, far_0, far_1, far_2, full,
-           shifted, acc, outgoing, incoming, load, first_s, first_r, own_s, own_r, far_s, far_r, full_r,
-           line_s, core_s, core_r, sum_s, sum_r):
+def kernel(order_hbm, counts_hbm, x_hbm, out_hbm, order, counts, x_ref, wide, gathered, first, far_0, far_1, far_2, full,
+           shifted, acc, outgoing, incoming, result, load, first_s, first_r, own_s, own_r, far_s, far_r, full_r,
+           line_s, core_s, core_r, sum_s, sum_r, out_s):
     far = (far_0, far_1, far_2)
     b = lax.axis_index("block")
     d = lax.axis_index("day")
@@ -52,12 +52,11 @@
     def day_at(k):
         return ((x + k) % NX) * 2 + yh
 
-    loads = [pltpu.make_async_copy(x_hbm.at[0], x_ref, load.at[0]),
-             pltpu.make_async_copy(order_hbm, order, load.at[1]),
-             pltpu.make_async_copy(counts_hbm, counts, load.at[2])]
-    for copy in loads:
-        copy.start()
-
+    loads = [pltpu.make_async_copy(
+        x_hbm.at[0, pl.ds(pl.multiple_of((x + k) % NX * 16, 16), 16)], x_ref.at[(x + k) % NX], load.at[n])
+        for n, k in enumerate((2, 1, 3, 0))]
+    loads += [pltpu.make_async_copy(order_hbm, order, load.at[NX]),
+              pltpu.make_async_copy(counts_hbm, counts, load.at[NX + 1])]
     barrier = pltpu.get_barrier_semaphore()
 
     def greet(device):
@@ -66,6 +65,8 @@
     spots = ((two, q), (two, p), (1, q), (-1, q), (1, p), (-1, p), (0, q))
     for j in (2, 1, 3):
         greet(at_device(CLASSES * j, p, d))
+    for copy in loads:
+        copy.start()
     for i, hop in enumerate((-two, -1, 1, 0)):
         for plane in range(PLANE):
             device = at_device(hop, plane, p * 2 + yh)
@@ -81,21 +82,8 @@
         greet(at_device(0, p, day_at(k)))
     greet(at_device(0, mate, d))
     greet(at_device(0, p, x * 2 + 1 - yh))
-    for copy in loads:
+    for copy in loads[NX:]:
         copy.wait()
-
-    rows = x_ref[...]
-    centered = rows - jnp.sum(rows, axis=1, keepdims=True) * (1.0 / SEG)
-    rms = jnp.sqrt(jnp.sum(centered * centered, axis=1, keepdims=True) * (1.0 / SEG) + 1e-05)
-    live = (lax.broadcasted_iota(jnp.int32, (CAP, 1), 0) < counts[b]).astype(F32)
-    wide[:, K - 128:] = jnp.zeros((CAP, 128), F32)
-    wide[:, :SEG] = jnp.clip(centered * (1.0 / rms), -CLIP, CLIP) * live
-    for g in range(NX):
-        for i in range(TILES):
-            gathered[x, g, i] = wide[16 * g:16 * g + 16, 128 * i:128 * i + 128].astype(BF16)
-        gathered[x, g, TILES] = jnp.zeros((16, 128), BF16)
-
-    pl.semaphore_wait(barrier, 31 - (p == x).astype(jnp.int32))
 
     hops = (0, 1, -1, two_x)
 
@@ -106,6 +94,24 @@
             first_s.at[i * NX + k], first_r.at[i * PLANE + p],
             device_id=at_device(hops[i], x, day_at(k)), device_id_type=MESH)
 
+    firsts = [(i, k) for k in (2, 1, 3, 0) for i in (3, 1, 2, 0) if i or k]
+    for n, k in enumerate((2, 1, 3, 0)):
+        g = (x + k) % NX
+        loads[n].wait()
+        rows = x_ref[g]
+        centered = rows - jnp.sum(rows, axis=1, keepdims=True) * (1.0 / SEG)
+        rms = jnp.sqrt(jnp.sum(centered * centered, axis=1, keepdims=True) * (1.0 / SEG) + 1e-05)
+        live = (16 * g + lax.broadcasted_iota(jnp.int32, (16, 1), 0) < counts[b]).astype(F32)
+        wide[:, K - 128:] = jnp.zeros((16, 128), F32)
+        wide[:, :SEG] = jnp.clip(centered * (1.0 / rms), -CLIP, CLIP) * live
+        for i in range(TILES):
+            gathered[x, g, i] = wide[:, 128 * i:128 * i + 128].astype(BF16)
+        gathered[x, g, TILES] = jnp.zeros((16, 128), BF16)
+
+    pl.semaphore_wait(barrier, 31 - (p == x).astype(jnp.int32))
+    for i, k in firsts:
+        first_copy(i, k).start()
+
     @pl.when(p != x)
     def _():
         first_copy(0, 0).start()
@@ -113,10 +119,6 @@
     @pl.when(p == x)
     def _():
         first[p] = gathered[x, x, pl.ds(mine * PER, PER)]
-
-    firsts = [(i, k) for k in (2, 1, 3, 0) for i in (3, 1, 2, 0) if i or k]
-    for i, k in firsts:
-        first_copy(i, k).start()
 
     def own_copy(k):
         return pltpu.make_async_remote_copy(
@@ -132,7 +134,7 @@
             for r in range(OWN_SHIFTS):
                 rolled = rows if r == 0 else pltpu.roll(rows, r, 1)
                 at = pl.multiple_of(r * CAP + g * 16, 16)
-                shifted[day, pl.ds(at, 16), :] = rolled
+                shifted[day % 2, pl.ds(at, 16), pl.ds(pl.multiple_of(day // 2 * K, 128), K)] = rolled
             return 0
         lax.fori_loop(0, CAP // 16, group, 0)
 
@@ -213,21 +215,23 @@
             core_copy(s, part).wait_recv()
 
     def add_days(s, part):
-        def one(k, _):
-            day = (part + 2 * k) % PLANE
+        odd = part % 2
+        left = []
+        for k in range(2):
             rows = jnp.concatenate(
-                [full[s, day, t // PER, t % PER] for t in range(TILES)], axis=1)
-            left = jnp.concatenate(
-                [pltpu.roll(rows, (HALF - OWN_SHIFTS * n) % K, 1) for n in range(OWNER_SHIFTS)], axis=0)
-            sums = lax.dot_general(left, shifted[day], (((1,), (1,)), ((), ())), preferred_element_type=F32)
-            acc[s] += sums
-            return 0
-        lax.fori_loop(0, 2, one, 0)
+                [full[s, odd + 2 * k, t // PER, t % PER] for t in range(TILES)], axis=1)
+            left.append(jnp.concatenate(
+                [pltpu.roll(rows, (HALF - OWN_SHIFTS * n) % K, 1) for n in range(OWNER_SHIFTS)], axis=0))
+        return lax.dot_general(jnp.concatenate(left, axis=1), shifted[odd], (((1,), (1,)), ((), ())),
+                               preferred_element_type=F32)
 
     def sum_copy(s):
         return pltpu.make_async_remote_copy(
             outgoing.at[s], incoming.at[s], sum_s.at[s], sum_r.at[s],
             device_id=at_device(0, p, x * 2 + 1 - yh), device_id_type=MESH)
+
+    def out_copy(s):
+        return pltpu.make_async_copy(result.at[s], out_hbm.at[s], out_s.at[s])
 
     def halves(s):
         whole = acc[s].reshape(OWNER_SHIFTS, 2, SHARE // 2, COLS)
@@ -241,28 +245,31 @@
     def finish(s):
         sum_copy(s).wait_recv()
         top, low = halves(s)
-        out_ref[s] = (jnp.where(yh == 0, top, low) + incoming[s].astype(F32)) * (float(DAYS * SEG) ** -0.5)
-
-    acc[...] = jnp.zeros_like(acc)
+        sums = (jnp.where(yh == 0, top, low) + incoming[s].astype(F32)) * (float(DAYS * SEG) ** -0.5)
+        for lag in range(LAGS):
+            n, r = lag // OWN_SHIFTS, lag % OWN_SHIFTS
+            result[s, lag] = sums[8 * n:8 * n + 8, CAP * r:CAP * r + CAP]
+        out_copy(s).start()
+
     open_owner(0)
     open_owner(1)
     own_shifts(1, 0)
     open_owner(2)
     lax.fori_loop(2, NX, own_shifts, 0)
     pass_on(0)
-    add_days(0, p)
+    acc[0] = add_days(0, p)
     pass_on(1)
     from_core(0)
-    add_days(0, mate)
+    acc[0] += add_days(0, mate)
     to_partner(0)
-    add_days(1, p)
+    acc[1] = add_days(1, p)
     pass_on(2)
     from_core(1)
-    add_days(1, mate)
+    acc[1] += add_days(1, mate)
     to_partner(1)
-    add_days(2, p)
+    acc[2] = add_days(2, p)
     from_core(2)
-    add_days(2, mate)
+    acc[2] += add_days(2, mate)
     to_partner(2)
 
     @pl.when(p != x)
@@ -282,6 +289,8 @@
     for s in range(STEPS):
         finish(s)
         sum_copy(s).wait_send()
+    for s in range(STEPS):
+        out_copy(s).wait()
 
 
 def per_device(traces, counts, order):
@@ -289,36 +298,35 @@
     tile = (16, 128)
     raw = pl.pallas_call(
         kernel,
-        out_shape=jax.ShapeDtypeStruct((STEPS, ROWS, COLS), F32),
+        out_shape=jax.ShapeDtypeStruct((STEPS, LAGS, SHARE // 2, CAP), F32),
         in_specs=[pl.BlockSpec(memory_space=pltpu.HBM)] * 3,
-        out_specs=pl.BlockSpec(memory_space=pltpu.VMEM),
+        out_specs=pl.BlockSpec(memory_space=pltpu.HBM),
         scratch_shapes=[
             pltpu.SMEM(order.shape, jnp.int32),
             pltpu.SMEM(counts.shape, jnp.int32),
-            pltpu.VMEM((CAP, SEG), F32),
-            pltpu.VMEM((CAP, K), F32),
+            pltpu.VMEM((NX, 16, SEG), F32),
+            pltpu.VMEM((16, K), F32),
             pltpu.VMEM((NX, NX, TILES + 1) + tile, BF16),
             pltpu.VMEM((CLASSES * PLANE, PER) + tile, BF16),
             pltpu.VMEM((CLASSES, PER) + tile, BF16),
             pltpu.VMEM((CLASSES, PER) + tile, BF16),
             pltpu.VMEM((CLASSES, PER) + tile, BF16),
             pltpu.VMEM((STEPS, PLANE, CLASSES, PER) + tile, BF16),
-            pltpu.VMEM((NX, COLS, K), BF16),
+            pltpu.VMEM((2, COLS, 2 * K), BF16),
             pltpu.VMEM((STEPS, 2 * ROWS, COLS), F32),
             pltpu.VMEM((STEPS, ROWS, COLS), BF16),
             pltpu.VMEM((STEPS, ROWS, COLS), BF16),
-            dma((3,)), dma((CLASSES * NX,)), dma((CLASSES * PLANE,)), dma((NX,)), dma((NX,)),
+            pltpu.VMEM((STEPS, LAGS, SHARE // 2, CAP), F32),
+            dma((NX + 2,)), dma((CLASSES * NX,)), dma((CLASSES * PLANE,)), dma((NX,)), dma((NX,)),
             dma((STEPS, CLASSES)), dma((STEPS, CLASSES)), dma((STEPS * PLANE, CLASSES)),
-            dma((STEPS, 7)), dma((STEPS, PLANE)), dma((STEPS, PLANE)), dma((STEPS,)), dma((STEPS,)),
+            dma((STEPS, 7)), dma((STEPS, PLANE)), dma((STEPS, PLANE)), dma((STEPS,)), dma((STEPS,)), dma((STEPS,)),
         ],
         compiler_params=pltpu.CompilerParams(
             collective_id=0, has_side_effects=True, vmem_limit_bytes=63 << 20),
         cost_estimate=pl.CostEstimate(flops=2 * STEPS * ROWS * COLS * K * DAYS, bytes_accessed=1 << 20, transcendentals=0),
         name="correlate",
     )(order, counts, traces)
-    parts = raw.reshape(STEPS, OWNER_SHIFTS, SHARE // 2, OWN_SHIFTS, CAP)
-    lags = parts.transpose(0, 2, 1, 3, 4).reshape(STEPS, SHARE // 2, OWNER_SHIFTS * OWN_SHIFTS, CAP)
-    return lags[:, :, :LAGS]
+    return raw.transpose(0, 2, 1, 3)
 
 
 def solution(mesh):

time: 56.6 us -> 57.4 us (1.014)
  Pallas kernels: 54.1 us -> 55.2 us
    unnamed x0 -> x1, local copies, waits for them, and re-layouts: none -> 2.04 us
    reshape x1 -> x0, local copies, waits for them, and re-layouts: 1.33 us -> none  [per_device(): parts = raw.reshape(STEPS, OWNER_SHIFTS, SHARE // 2, OWN_SHIFTS, CAP)]
    pallas_call x1, Pallas kernels: 54.1 us -> 55.2 us  [per_device(): pl.pallas_call(kernel, out_shape=jax.ShapeDtypeStruct((STEPS, LAGS, SHARE...]
    slice x1 -> x0, local copies, waits for them, and re-layouts: 0.92 us -> none  [per_device(): return lags[:, :, :LAGS]]
where the time goes in v4:
time: 57.4 us; the launch traced here: 57.2 us
  Pallas kernels  55.2 us (96%)
  local copies, waits for them, and re-layouts  2.04 us (4%)
    pallas_call x1, Pallas kernels, per_device(): pl.pallas_call(kernel, out_shape=jax.ShapeDtypeStruct((STEPS, LAGS, SHARE...  55.2 us
    unnamed x1, local copies, waits for them, and re-layouts  2.04 us

profile of v4, /device:TPU:1, one launch (start us, length us, event | category | flops | bytes accessed | tf_op | source)
XLA Modules:
  0.0 57.2 jit_solution(5689942366599216881)
XLA Ops:
  0.0 55.2 %correlate.1 = f32[3,61,8,64]{3,2,1,0:T(8,128)} custom-call(s32[64]{0:T(128)} %order_hbm.1, s32[64]{0:T(128)} %counts_hbm.1, f32[1,64,2400]{2,1,0:T(8,128)} %x_hbm.1), custom_call_target="tpu_custom_call" | custom-call | flops 3825205248 | bytes 1048576 | tf_op jit(solution)/shard_map/correlate/pallas_call | solution.py:299
  55.2 2.0 %copy.5 = f32[3,8,61,64]{3,1,2,0:T(8,128)} copy(f32[3,8,61,64]{3,1,2,0:T(8,128)} %bitcast.1) | data formatting | bytes 749568

commit v5 on v4

--- a/solution.py
+++ b/solution.py
@@ -32,7 +32,7 @@
 
 def kernel(order_hbm, counts_hbm, x_hbm, out_hbm, order, counts, x_ref, wide, gathered, first, far_0, far_1, far_2, full,
            shifted, acc, outgoing, incoming, result, load, first_s, first_r, own_s, own_r, far_s, far_r, full_r,
-           line_s, core_s, core_r, sum_s, sum_r, out_s):
+           line_s, core_s, core_r, sum_s, sum_r, out_s, token):
     far = (far_0, far_1, far_2)
     b = lax.axis_index("block")
     d = lax.axis_index("day")
@@ -63,7 +63,7 @@
         pl.semaphore_signal(barrier, 1, device_id=device, device_id_type=MESH)
 
     spots = ((two, q), (two, p), (1, q), (-1, q), (1, p), (-1, p), (0, q))
-    for j in (2, 1, 3):
+    for j in (1, 3):
         greet(at_device(CLASSES * j, p, d))
     for copy in loads:
         copy.start()
@@ -108,7 +108,8 @@
             gathered[x, g, i] = wide[:, 128 * i:128 * i + 128].astype(BF16)
         gathered[x, g, TILES] = jnp.zeros((16, 128), BF16)
 
-    pl.semaphore_wait(barrier, 31 - (p == x).astype(jnp.int32))
+    pl.semaphore_wait(barrier, 30 - (p == x).astype(jnp.int32))
+    pl.semaphore_signal(token, 1, device_id=at_device(-CLASSES, p, d), device_id_type=MESH)
     for i, k in firsts:
         first_copy(i, k).start()
 
@@ -159,6 +160,7 @@
             far[s].at[z // CLASSES], far[s].at[z // CLASSES], far_s.at[s, j], far_r.at[s, z // CLASSES],
             device_id=at_device(CLASSES * j, p, d), device_id_type=MESH)
 
+    pl.semaphore_wait(token, 1)
     for s in range(STEPS):
         gap = (z - order[s] // PLANE + NZ) % NZ
         came = jnp.where(gap == 1, 1, jnp.where(gap == NZ - 1, 2, jnp.where(gap == (two + NZ) % NZ, 3, 0)))
@@ -272,6 +274,8 @@
     acc[2] += add_days(2, mate)
     to_partner(2)
 
+    finish(0)
+
     @pl.when(p != x)
     def _():
         first_copy(0, 0).wait_send()
@@ -279,6 +283,7 @@
         first_copy(i, k).wait_send()
     for k in range(1, NX):
         own_copy(k).wait_send()
+    finish(1)
     for s in range(STEPS):
         for k in range(1, NX):
             far_copy(s, k).wait_send()
@@ -286,10 +291,9 @@
             spread(s, j).wait_send()
         for part in (p, q):
             core_copy(s, part).wait_send()
+    finish(2)
     for s in range(STEPS):
-        finish(s)
         sum_copy(s).wait_send()
-    for s in range(STEPS):
         out_copy(s).wait()
 
 
@@ -320,6 +324,7 @@
             dma((NX + 2,)), dma((CLASSES * NX,)), dma((CLASSES * PLANE,)), dma((NX,)), dma((NX,)),
             dma((STEPS, CLASSES)), dma((STEPS, CLASSES)), dma((STEPS * PLANE, CLASSES)),
             dma((STEPS, 7)), dma((STEPS, PLANE)), dma((STEPS, PLANE)), dma((STEPS,)), dma((STEPS,)), dma((STEPS,)),
+            pltpu.SemaphoreType.REGULAR,
         ],
         compiler_params=pltpu.CompilerParams(
             collective_id=0, has_side_effects=True, vmem_limit_bytes=63 << 20),

time: 57.4 us -> 57.5 us (level)
  the two profiles are of different devices: /device:TPU:1 before, /device:TPU:4 now
where the time goes in v5:
time: 57.5 us; the launch traced here: 57.3 us
  Pallas kernels  55.3 us (96%)
  local copies, waits for them, and re-layouts  2.04 us (4%)
    pallas_call x1, Pallas kernels, per_device(): pl.pallas_call(kernel, out_shape=jax.ShapeDtypeStruct((STEPS, LAGS, SHARE...  55.3 us
    unnamed x1, local copies, waits for them, and re-layouts  2.04 us

profile of v5, /device:TPU:4, one launch (start us, length us, event | category | flops | bytes accessed | tf_op | source)
XLA Modules:
  0.0 57.3 jit_solution(11669366905679142648)
XLA Ops:
  0.0 55.3 %correlate.1 = f32[3,61,8,64]{3,2,1,0:T(8,128)} custom-call(s32[64]{0:T(128)} %order_hbm.1, s32[64]{0:T(128)} %counts_hbm.1, f32[1,64,2400]{2,1,0:T(8,128)} %x_hbm.1), custom_call_target="tpu_custom_call" | custom-call | flops 3825205248 | bytes 1048576 | tf_op jit(solution)/shard_map/correlate/pallas_call | solution.py:303
  55.3 2.0 %copy.5 = f32[3,8,61,64]{3,1,2,0:T(8,128)} copy(f32[3,8,61,64]{3,1,2,0:T(8,128)} %bitcast.1) | data formatting | bytes 749568

commit v6 on v5

--- a/solution.py
+++ b/solution.py
@@ -30,10 +30,9 @@
 BF16 = jnp.bfloat16
 
 
-def kernel(order_hbm, counts_hbm, x_hbm, out_hbm, order, counts, x_ref, wide, gathered, first, far_0, far_1, far_2, full,
+def kernel(order_hbm, counts_hbm, x_hbm, out_hbm, order, counts, x_ref, wide, gathered, first, far, full,
            shifted, acc, outgoing, incoming, result, load, first_s, first_r, own_s, own_r, far_s, far_r, full_r,
            line_s, core_s, core_r, sum_s, sum_r, out_s, token):
-    far = (far_0, far_1, far_2)
     b = lax.axis_index("block")
     d = lax.axis_index("day")
     z = b // PLANE
@@ -47,16 +46,25 @@
     mate = p + 1 - 2 * (p % 2)
 
     def at_device(hop, plane, day):
-        return ((z + hop + NZ) % NZ) * PLANE + plane, day
+        return lax.rem(z + hop + NZ, NZ) * PLANE + plane, day
 
     def day_at(k):
-        return ((x + k) % NX) * 2 + yh
-
-    loads = [pltpu.make_async_copy(
-        x_hbm.at[0, pl.ds(pl.multiple_of((x + k) % NX * 16, 16), 16)], x_ref.at[(x + k) % NX], load.at[n])
-        for n, k in enumerate((2, 1, 3, 0))]
-    loads += [pltpu.make_async_copy(order_hbm, order, load.at[NX]),
-              pltpu.make_async_copy(counts_hbm, counts, load.at[NX + 1])]
+        return lax.rem(x + k, NX) * 2 + yh
+
+    def each(low, high, step):
+        def body(n, _):
+            step(n)
+            return 0
+        lax.fori_loop(low, high, body, 0)
+
+    def load_rows(n):
+        g = lax.rem(x + 1 + n, NX)
+        return pltpu.make_async_copy(
+            x_hbm.at[0, pl.ds(pl.multiple_of(g * 16, 16), 16)], x_ref.at[g], load.at[n])
+
+    loads = [pltpu.make_async_copy(order_hbm, order, load.at[NX]),
+             pltpu.make_async_copy(counts_hbm, counts, load.at[NX + 1])]
+
     barrier = pltpu.get_barrier_semaphore()
 
     def greet(device):
@@ -65,39 +73,39 @@
     spots = ((two, q), (two, p), (1, q), (-1, q), (1, p), (-1, p), (0, q))
     for j in (1, 3):
         greet(at_device(CLASSES * j, p, d))
+    each(0, NX, lambda n: load_rows(n).start())
     for copy in loads:
         copy.start()
-    for i, hop in enumerate((-two, -1, 1, 0)):
-        for plane in range(PLANE):
-            device = at_device(hop, plane, p * 2 + yh)
-            if i < 3:
-                greet(device)
-            else:
-                @pl.when(jnp.logical_or(plane != p, p != x))
-                def _():
-                    greet(device)
+
+    def greet_sources(plane):
+        for hop in (-two, -1, 1):
+            greet(at_device(hop, plane, p * 2 + yh))
+
+        @pl.when(jnp.logical_or(plane != p, p != x))
+        def _():
+            greet(at_device(0, plane, p * 2 + yh))
+
+    each(0, PLANE, greet_sources)
     for hop, plane in spots:
         greet(at_device(-hop, plane, d))
-    for k in range(1, NX):
-        greet(at_device(0, p, day_at(k)))
+    each(1, NX, lambda k: greet(at_device(0, p, day_at(k))))
     greet(at_device(0, mate, d))
     greet(at_device(0, p, x * 2 + 1 - yh))
-    for copy in loads[NX:]:
+    for copy in loads:
         copy.wait()
 
     hops = (0, 1, -1, two_x)
 
     def first_copy(i, k):
-        to_class = (z + hops[i] + NZ) % CLASSES
-        return pltpu.make_async_remote_copy(
-            gathered.at[x, (x + k) % NX, pl.ds(to_class * PER, PER)], first.at[i * PLANE + p],
+        to_class = lax.rem(z + hops[i] + NZ, CLASSES)
+        return pltpu.make_async_remote_copy(
+            gathered.at[x, lax.rem(x + k, NX), pl.ds(to_class * PER, PER)], first.at[i * PLANE + p],
             first_s.at[i * NX + k], first_r.at[i * PLANE + p],
             device_id=at_device(hops[i], x, day_at(k)), device_id_type=MESH)
 
-    firsts = [(i, k) for k in (2, 1, 3, 0) for i in (3, 1, 2, 0) if i or k]
-    for n, k in enumerate((2, 1, 3, 0)):
-        g = (x + k) % NX
-        loads[n].wait()
+    def whiten(n):
+        g = lax.rem(x + 1 + n, NX)
+        load_rows(n).wait()
         rows = x_ref[g]
         centered = rows - jnp.sum(rows, axis=1, keepdims=True) * (1.0 / SEG)
         rms = jnp.sqrt(jnp.sum(centered * centered, axis=1, keepdims=True) * (1.0 / SEG) + 1e-05)
@@ -108,14 +116,20 @@
             gathered[x, g, i] = wide[:, 128 * i:128 * i + 128].astype(BF16)
         gathered[x, g, TILES] = jnp.zeros((16, 128), BF16)
 
+    each(0, NX, whiten)
     pl.semaphore_wait(barrier, 30 - (p == x).astype(jnp.int32))
     pl.semaphore_signal(token, 1, device_id=at_device(-CLASSES, p, d), device_id_type=MESH)
-    for i, k in firsts:
-        first_copy(i, k).start()
-
-    @pl.when(p != x)
-    def _():
-        first_copy(0, 0).start()
+
+    def send_first(n):
+        k = lax.rem(n + 2, NX)
+        for i in (3, 1, 2):
+            first_copy(i, k).start()
+
+        @pl.when(jnp.logical_or(k != 0, p != x))
+        def _():
+            first_copy(0, k).start()
+
+    each(0, NX, send_first)
 
     @pl.when(p == x)
     def _():
@@ -126,8 +140,7 @@
             gathered.at[x], gathered.at[x], own_s.at[k], own_r.at[x],
             device_id=at_device(0, p, day_at(k)), device_id_type=MESH)
 
-    for k in (1, 3, 2):
-        own_copy(k).start()
+    each(1, NX, lambda k: own_copy(k).start())
 
     def shifts_of_day(day):
         def group(g, _):
@@ -139,34 +152,38 @@
             return 0
         lax.fori_loop(0, CAP // 16, group, 0)
 
-    def own_shifts(k, _):
-        day = (x + NX - k) % NX
+    def own_shifts(k):
+        day = lax.rem(x + NX - k, NX)
         pltpu.make_async_remote_copy(
             gathered.at[day], gathered.at[day], own_s.at[k], own_r.at[day],
             device_id=(b, d), device_id_type=MESH).wait_recv()
         shifts_of_day(day)
-        return 0
 
     shifts_of_day(x)
-    for j in range(CLASSES * PLANE):
+
+    def wait_first(j):
         @pl.when(jnp.logical_or(p != x, p != j))
         def _():
             pltpu.make_async_remote_copy(
                 first.at[j], first.at[j], first_s.at[0], first_r.at[j],
                 device_id=(b, d), device_id_type=MESH).wait_recv()
 
+    each(0, CLASSES * PLANE, wait_first)
+
     def far_copy(s, j):
         return pltpu.make_async_remote_copy(
-            far[s].at[z // CLASSES], far[s].at[z // CLASSES], far_s.at[s, j], far_r.at[s, z // CLASSES],
+            far.at[s, z // CLASSES], far.at[s, z // CLASSES], far_s.at[s, j], far_r.at[s, z // CLASSES],
             device_id=at_device(CLASSES * j, p, d), device_id_type=MESH)
 
     pl.semaphore_wait(token, 1)
-    for s in range(STEPS):
+    def send_far(s):
         gap = (z - order[s] // PLANE + NZ) % NZ
         came = jnp.where(gap == 1, 1, jnp.where(gap == NZ - 1, 2, jnp.where(gap == (two + NZ) % NZ, 3, 0)))
-        far[s][z // CLASSES] = first[came * PLANE + order[s] % PLANE]
+        far[s, z // CLASSES] = first[came * PLANE + order[s] % PLANE]
         for j in (2, 1, 3):
             far_copy(s, j).start()
+
+    each(0, STEPS, send_far)
 
     def piece(s, part, cls, sem, to):
         return pltpu.make_async_remote_copy(
@@ -187,19 +204,22 @@
             full.at[s, part], full.at[s, part], core_s.at[s, part], core_r.at[s, part],
             device_id=core, device_id_type=MESH)
 
-    others = [(z + k + NZ) % CLASSES for k in (1, 3, 2)]
+    others = [lax.rem(z + k, CLASSES) for k in (1, 3, 2)]
 
     def open_owner(s):
         for j in (1, 3, 2):
-            src = (z // CLASSES + j) % CLASSES
+            src = lax.rem(z // CLASSES + j, CLASSES)
             pltpu.make_async_remote_copy(
-                far[s].at[src], far[s].at[src], far_s.at[s, j], far_r.at[s, src],
+                far.at[s, src], far.at[s, src], far_s.at[s, j], far_r.at[s, src],
                 device_id=(b, d), device_id_type=MESH).wait_recv()
         owner_z = order[s] // PLANE
         gap = (mine - owner_z + NZ) % CLASSES
         step = jnp.where(gap == 3, -1, jnp.where(gap == 2, two, gap))
         sender = (owner_z + step + NZ) % NZ
-        full[s, p, mine] = far[s][sender // CLASSES]
+        best = far[s, 0]
+        for n in range(1, CLASSES):
+            best = jnp.where(sender // CLASSES == n, far[s, n], best)
+        full[s, p, mine] = best
         for j in range(len(spots)):
             spread(s, j).start()
 
@@ -216,8 +236,7 @@
         for part in (mate, (mate + 2) % PLANE):
             core_copy(s, part).wait_recv()
 
-    def add_days(s, part):
-        odd = part % 2
+    def add_days(s, odd):
         left = []
         for k in range(2):
             rows = jnp.concatenate(
@@ -253,48 +272,61 @@
             result[s, lag] = sums[8 * n:8 * n + 8, CAP * r:CAP * r + CAP]
         out_copy(s).start()
 
-    open_owner(0)
-    open_owner(1)
-    own_shifts(1, 0)
-    open_owner(2)
-    lax.fori_loop(2, NX, own_shifts, 0)
+    each(0, STEPS, open_owner)
+    each(1, NX, own_shifts)
     pass_on(0)
-    acc[0] = add_days(0, p)
-    pass_on(1)
-    from_core(0)
-    acc[0] += add_days(0, mate)
-    to_partner(0)
-    acc[1] = add_days(1, p)
-    pass_on(2)
-    from_core(1)
-    acc[1] += add_days(1, mate)
-    to_partner(1)
-    acc[2] = add_days(2, p)
-    from_core(2)
-    acc[2] += add_days(2, mate)
-    to_partner(2)
-
-    finish(0)
-
-    @pl.when(p != x)
-    def _():
-        first_copy(0, 0).wait_send()
-    for i, k in firsts:
-        first_copy(i, k).wait_send()
-    for k in range(1, NX):
-        own_copy(k).wait_send()
-    finish(1)
-    for s in range(STEPS):
+
+    def owner(s):
+        def part(h):
+            @pl.when(h == 1)
+            def _():
+                @pl.when(s < STEPS - 1)
+                def _():
+                    pass_on(s + 1)
+                from_core(s)
+            sums = add_days(s, lax.rem(p + h, 2))
+
+            @pl.when(h == 0)
+            def _():
+                acc[s] = sums
+
+            @pl.when(h == 1)
+            def _():
+                acc[s] += sums
+        each(0, 2, part)
+        to_partner(s)
+
+    each(0, STEPS, owner)
+
+    def sent(k):
+        for i in range(1, CLASSES):
+            first_copy(i, k).wait_send()
+
+        @pl.when(jnp.logical_or(k != 0, p != x))
+        def _():
+            first_copy(0, k).wait_send()
+
+        @pl.when(k > 0)
+        def _():
+            own_copy(k).wait_send()
+
+    def owner_sent(s):
         for k in range(1, NX):
             far_copy(s, k).wait_send()
         for j in range(len(spots)):
             spread(s, j).wait_send()
         for part in (p, q):
             core_copy(s, part).wait_send()
-    finish(2)
-    for s in range(STEPS):
+
+    each(0, NX, sent)
+    each(0, STEPS, owner_sent)
+    each(0, STEPS, finish)
+
+    def done(s):
         sum_copy(s).wait_send()
         out_copy(s).wait()
+
+    each(0, STEPS, done)
 
 
 def per_device(traces, counts, order):
@@ -312,9 +344,7 @@
             pltpu.VMEM((16, K), F32),
             pltpu.VMEM((NX, NX, TILES + 1) + tile, BF16),
             pltpu.VMEM((CLASSES * PLANE, PER) + tile, BF16),
-            pltpu.VMEM((CLASSES, PER) + tile, BF16),
-            pltpu.VMEM((CLASSES, PER) + tile, BF16),
-            pltpu.VMEM((CLASSES, PER) + tile, BF16),
+            pltpu.VMEM((STEPS, CLASSES, PER) + tile, BF16),
             pltpu.VMEM((STEPS, PLANE, CLASSES, PER) + tile, BF16),
             pltpu.VMEM((2, COLS, 2 * K), BF16),
             pltpu.VMEM((STEPS, 2 * ROWS, COLS), F32),

time: 57.5 us -> 55.6 us (0.967)
  the two profiles are of different devices: /device:TPU:4 before, /device:TPU:6 now
where the time goes in v6:
time: 55.6 us; the launch traced here: 55.4 us
  Pallas kernels  53.4 us (96%)
  local copies, waits for them, and re-layouts  2.04 us (4%)
    pallas_call x1, Pallas kernels, per_device(): pl.pallas_call(kernel, out_shape=jax.ShapeDtypeStruct((STEPS, LAGS, SHARE...  53.4 us
    unnamed x1, local copies, waits for them, and re-layouts  2.04 us

profile of v6, /device:TPU:6, one launch (start us, length us, event | category | flops | bytes accessed | tf_op | source)
XLA Modules:
  0.0 55.4 jit_solution(7896575334048547809)
XLA Ops:
  0.0 53.4 %correlate.1 = f32[3,61,8,64]{3,2,1,0:T(8,128)} custom-call(s32[64]{0:T(128)} %order_hbm.1, s32[64]{0:T(128)} %counts_hbm.1, f32[1,64,2400]{2,1,0:T(8,128)} %x_hbm.1), custom_call_target="tpu_custom_call" | custom-call | flops 3825205248 | bytes 1048576 | tf_op jit(solution)/shard_map/correlate/pallas_call | solution.py:335
  53.4 2.0 %copy.5 = f32[3,8,61,64]{3,1,2,0:T(8,128)} copy(f32[3,8,61,64]{3,1,2,0:T(8,128)} %bitcast.1) | data formatting | bytes 749568

commit v7 on v6

--- a/solution.py
+++ b/solution.py
@@ -58,7 +58,7 @@
         lax.fori_loop(low, high, body, 0)
 
     def load_rows(n):
-        g = lax.rem(x + 1 + n, NX)
+        g = lax.rem(x + 2 + n, NX)
         return pltpu.make_async_copy(
             x_hbm.at[0, pl.ds(pl.multiple_of(g * 16, 16), 16)], x_ref.at[g], load.at[n])
 
@@ -104,7 +104,7 @@
             device_id=at_device(hops[i], x, day_at(k)), device_id_type=MESH)
 
     def whiten(n):
-        g = lax.rem(x + 1 + n, NX)
+        g = lax.rem(x + 2 + n, NX)
         load_rows(n).wait()
         rows = x_ref[g]
         centered = rows - jnp.sum(rows, axis=1, keepdims=True) * (1.0 / SEG)
@@ -116,11 +116,14 @@
             gathered[x, g, i] = wide[:, 128 * i:128 * i + 128].astype(BF16)
         gathered[x, g, TILES] = jnp.zeros((16, 128), BF16)
 
-    each(0, NX, whiten)
-    pl.semaphore_wait(barrier, 30 - (p == x).astype(jnp.int32))
-    pl.semaphore_signal(token, 1, device_id=at_device(-CLASSES, p, d), device_id_type=MESH)
-
     def send_first(n):
+        whiten(n)
+
+        @pl.when(n == 0)
+        def _():
+            pl.semaphore_wait(barrier, 30 - (p == x).astype(jnp.int32))
+            pl.semaphore_signal(token, 1, device_id=at_device(-CLASSES, p, d), device_id_type=MESH)
+
         k = lax.rem(n + 2, NX)
         for i in (3, 1, 2):
             first_copy(i, k).start()
@@ -266,7 +269,7 @@
     def finish(s):
         sum_copy(s).wait_recv()
         top, low = halves(s)
-        sums = (jnp.where(yh == 0, top, low) + incoming[s].astype(F32)) * (float(DAYS * SEG) ** -0.5)
+        sums = jnp.where(yh == 0, top, low) + incoming[s].astype(F32)
         for lag in range(LAGS):
             n, r = lag // OWN_SHIFTS, lag % OWN_SHIFTS
             result[s, lag] = sums[8 * n:8 * n + 8, CAP * r:CAP * r + CAP]
@@ -361,7 +364,7 @@
         cost_estimate=pl.CostEstimate(flops=2 * STEPS * ROWS * COLS * K * DAYS, bytes_accessed=1 << 20, transcendentals=0),
         name="correlate",
     )(order, counts, traces)
-    return raw.transpose(0, 2, 1, 3)
+    return raw.transpose(0, 2, 1, 3) * (float(DAYS * SEG) ** -0.5)
 
 
 def solution(mesh):

time: 55.6 us -> 55.6 us (level)
  other arithmetic: 0 us -> 2.05 us
  local copies, waits for them, and re-layouts: 2.04 us -> 0 us
    mul x0 -> x1, other arithmetic: none -> 2.05 us  [per_device(): return raw.transpose(0, 2, 1, 3) * float(DAYS * SEG) ** (-0.5)]
    unnamed x1 -> x0, local copies, waits for them, and re-layouts: 2.04 us -> none
where the time goes in v7:
time: 55.6 us; the launch traced here: 55.5 us
  Pallas kernels  53.4 us (96%)
  other arithmetic  2.05 us (4%)
    pallas_call x1, Pallas kernels, per_device(): pl.pallas_call(kernel, out_shape=jax.ShapeDtypeStruct((STEPS, LAGS, SHARE...  53.4 us
    mul x1, other arithmetic, per_device(): return raw.transpose(0, 2, 1, 3) * float(DAYS * SEG) ** (-0.5)  2.05 us

profile of v7, /device:TPU:6, one launch (start us, length us, event | category | flops | bytes accessed | tf_op | source)
XLA Modules:
  0.0 55.5 jit_solution(3573622960759451950)
XLA Ops:
  0.0 53.4 %correlate.1 = f32[3,61,8,64]{3,2,1,0:T(8,128)} custom-call(s32[64]{0:T(128)} %order_hbm.1, s32[64]{0:T(128)} %counts_hbm.1, f32[1,64,2400]{2,1,0:T(8,128)} %x_hbm.1), custom_call_target="tpu_custom_call" | custom-call | flops 3825205248 | bytes 1048576 | tf_op jit(solution)/shard_map/correlate/pallas_call | solution.py:338
  53.4 2.1 %multiply_bitcast_fusion = f32[3,8,61,64]{3,1,2,0:T(8,128)} fusion(f32[3,61,8,64]{3,2,1,0:T(8,128)} %correlate.1), kind=kLoop, calls=%fused_computation | loop fusion | flops 93696 | bytes 749568 | tf_op jit(solution)/shard_map/mul | solution.py:367

commit v8 on v6

--- a/solution.py
+++ b/solution.py
@@ -14,6 +14,7 @@
 CAP = 64
 CLIP = 2.5
 DAYS = 8
+N_BLOCK = 64
 NZ = 16
 NX = 4
 PLANE = 4
@@ -30,7 +31,7 @@
 BF16 = jnp.bfloat16
 
 
-def kernel(order_hbm, counts_hbm, x_hbm, out_hbm, order, counts, x_ref, wide, gathered, first, far, full,
+def kernel(table_hbm, x_hbm, out_hbm, table, x_ref, wide, gathered, first, far, full,
            shifted, acc, outgoing, incoming, result, load, first_s, first_r, own_s, own_r, far_s, far_r, full_r,
            line_s, core_s, core_r, sum_s, sum_r, out_s, token):
     b = lax.axis_index("block")
@@ -62,8 +63,7 @@
         return pltpu.make_async_copy(
             x_hbm.at[0, pl.ds(pl.multiple_of(g * 16, 16), 16)], x_ref.at[g], load.at[n])
 
-    loads = [pltpu.make_async_copy(order_hbm, order, load.at[NX]),
-             pltpu.make_async_copy(counts_hbm, counts, load.at[NX + 1])]
+    load_table = pltpu.make_async_copy(table_hbm, table, load.at[NX])
 
     barrier = pltpu.get_barrier_semaphore()
 
@@ -74,8 +74,7 @@
     for j in (1, 3):
         greet(at_device(CLASSES * j, p, d))
     each(0, NX, lambda n: load_rows(n).start())
-    for copy in loads:
-        copy.start()
+    load_table.start()
 
     def greet_sources(plane):
         for hop in (-two, -1, 1):
@@ -91,8 +90,7 @@
     each(1, NX, lambda k: greet(at_device(0, p, day_at(k))))
     greet(at_device(0, mate, d))
     greet(at_device(0, p, x * 2 + 1 - yh))
-    for copy in loads:
-        copy.wait()
+    load_table.wait()
 
     hops = (0, 1, -1, two_x)
 
@@ -109,7 +107,7 @@
         rows = x_ref[g]
         centered = rows - jnp.sum(rows, axis=1, keepdims=True) * (1.0 / SEG)
         rms = jnp.sqrt(jnp.sum(centered * centered, axis=1, keepdims=True) * (1.0 / SEG) + 1e-05)
-        live = (16 * g + lax.broadcasted_iota(jnp.int32, (16, 1), 0) < counts[b]).astype(F32)
+        live = (16 * g + lax.broadcasted_iota(jnp.int32, (16, 1), 0) < table[b]).astype(F32)
         wide[:, K - 128:] = jnp.zeros((16, 128), F32)
         wide[:, :SEG] = jnp.clip(centered * (1.0 / rms), -CLIP, CLIP) * live
         for i in range(TILES):
@@ -177,9 +175,9 @@
 
     pl.semaphore_wait(token, 1)
     def send_far(s):
-        gap = (z - order[s] // PLANE + NZ) % NZ
+        gap = (z - table[N_BLOCK + s] // PLANE + NZ) % NZ
         came = jnp.where(gap == 1, 1, jnp.where(gap == NZ - 1, 2, jnp.where(gap == (two + NZ) % NZ, 3, 0)))
-        far[s, z // CLASSES] = first[came * PLANE + order[s] % PLANE]
+        far[s, z // CLASSES] = first[came * PLANE + table[N_BLOCK + s] % PLANE]
         for j in (2, 1, 3):
             far_copy(s, j).start()
 
@@ -212,7 +210,7 @@
             pltpu.make_async_remote_copy(
                 far.at[s, src], far.at[s, src], far_s.at[s, j], far_r.at[s, src],
                 device_id=(b, d), device_id_type=MESH).wait_recv()
-        owner_z = order[s] // PLANE
+        owner_z = table[N_BLOCK + s] // PLANE
         gap = (mine - owner_z + NZ) % CLASSES
         step = jnp.where(gap == 3, -1, jnp.where(gap == 2, two, gap))
         sender = (owner_z + step + NZ) % NZ
@@ -252,24 +250,28 @@
             device_id=at_device(0, p, x * 2 + 1 - yh), device_id_type=MESH)
 
     def out_copy(s):
-        return pltpu.make_async_copy(result.at[s], out_hbm.at[s], out_s.at[s])
-
-    def halves(s):
-        whole = acc[s].reshape(OWNER_SHIFTS, 2, SHARE // 2, COLS)
-        return whole[:, 0].reshape(ROWS, COLS), whole[:, 1].reshape(ROWS, COLS)
+        return pltpu.make_async_copy(result.at[s, pl.ds(0, LAGS)], out_hbm.at[s], out_s.at[s])
+
+    def half_rows(s, n, half):
+        return acc[s, pl.ds(pl.multiple_of(16 * n + 8 * half, 8), 8), :]
 
     def to_partner(s):
-        top, low = halves(s)
-        outgoing[s] = jnp.where(yh == 0, low, top).astype(BF16)
+        def pair(n):
+            rows = jnp.concatenate([half_rows(s, 2 * n, 1 - yh), half_rows(s, 2 * n + 1, 1 - yh)], axis=0)
+            outgoing[s, pl.ds(pl.multiple_of(16 * n, 16), 16), :] = rows.astype(BF16)
+        each(0, OWNER_SHIFTS // 2, pair)
         sum_copy(s).start()
 
     def finish(s):
         sum_copy(s).wait_recv()
-        top, low = halves(s)
-        sums = (jnp.where(yh == 0, top, low) + incoming[s].astype(F32)) * (float(DAYS * SEG) ** -0.5)
-        for lag in range(LAGS):
-            n, r = lag // OWN_SHIFTS, lag % OWN_SHIFTS
-            result[s, lag] = sums[8 * n:8 * n + 8, CAP * r:CAP * r + CAP]
+
+        def pair(n):
+            got = incoming[s, pl.ds(pl.multiple_of(16 * n, 16), 16), :].astype(F32)
+            for k in range(2):
+                sums = (half_rows(s, 2 * n + k, yh) + got[8 * k:8 * k + 8]) * (float(DAYS * SEG) ** -0.5)
+                for r in range(OWN_SHIFTS):
+                    result[s, OWN_SHIFTS * (2 * n + k) + r] = sums[:, CAP * r:CAP * r + CAP]
+        each(0, OWNER_SHIFTS // 2, pair)
         out_copy(s).start()
 
     each(0, STEPS, open_owner)
@@ -335,11 +337,10 @@
     raw = pl.pallas_call(
         kernel,
         out_shape=jax.ShapeDtypeStruct((STEPS, LAGS, SHARE // 2, CAP), F32),
-        in_specs=[pl.BlockSpec(memory_space=pltpu.HBM)] * 3,
+        in_specs=[pl.BlockSpec(memory_space=pltpu.HBM)] * 2,
         out_specs=pl.BlockSpec(memory_space=pltpu.HBM),
         scratch_shapes=[
-            pltpu.SMEM(order.shape, jnp.int32),
-            pltpu.SMEM(counts.shape, jnp.int32),
+            pltpu.SMEM((2 * N_BLOCK,), jnp.int32),
             pltpu.VMEM((NX, 16, SEG), F32),
             pltpu.VMEM((16, K), F32),
             pltpu.VMEM((NX, NX, TILES + 1) + tile, BF16),
@@ -350,17 +351,17 @@
             pltpu.VMEM((STEPS, 2 * ROWS, COLS), F32),
             pltpu.VMEM((STEPS, ROWS, COLS), BF16),
             pltpu.VMEM((STEPS, ROWS, COLS), BF16),
-            pltpu.VMEM((STEPS, LAGS, SHARE // 2, CAP), F32),
-            dma((NX + 2,)), dma((CLASSES * NX,)), dma((CLASSES * PLANE,)), dma((NX,)), dma((NX,)),
+            pltpu.VMEM((STEPS, OWN_SHIFTS * OWNER_SHIFTS, SHARE // 2, CAP), F32),
+            dma((NX + 1,)), dma((CLASSES * NX,)), dma((CLASSES * PLANE,)), dma((NX,)), dma((NX,)),
             dma((STEPS, CLASSES)), dma((STEPS, CLASSES)), dma((STEPS * PLANE, CLASSES)),
             dma((STEPS, 7)), dma((STEPS, PLANE)), dma((STEPS, PLANE)), dma((STEPS,)), dma((STEPS,)), dma((STEPS,)),
             pltpu.SemaphoreType.REGULAR,
         ],
         compiler_params=pltpu.CompilerParams(
-            collective_id=0, has_side_effects=True, vmem_limit_bytes=63 << 20),
+            collective_id=0, has_side_effects=True, vmem_limit_bytes=48 << 20),
         cost_estimate=pl.CostEstimate(flops=2 * STEPS * ROWS * COLS * K * DAYS, bytes_accessed=1 << 20, transcendentals=0),
         name="correlate",
-    )(order, counts, traces)
+    )(jnp.concatenate([counts, order]), traces)
     return raw.transpose(0, 2, 1, 3)
 
 

time: 55.6 us -> 57.3 us (1.031); the launches traced: 55.4 us -> 56.3 us
  other arithmetic: 0 us -> 0.75 us
    concatenate x0 -> x1, other arithmetic: none -> 0.75 us  [per_device(): jnp.concatenate([counts, order])]
    unnamed x1 -> x3, local copies, waits for them, and re-layouts: 2.04 us -> 1.95 us
where the time goes in v8:
time: 57.3 us; the launch traced here: 56.3 us
  Pallas kernels  53.6 us (94%)
  local copies, waits for them, and re-layouts  1.95 us (3%)
  other arithmetic  0.75 us (1%)
    pallas_call x1, Pallas kernels, per_device(): pl.pallas_call(kernel, out_shape=jax.ShapeDtypeStruct((STEPS, LAGS, SHARE...  53.6 us
    unnamed x3, local copies, waits for them, and re-layouts  1.95 us

profile of v8, /device:TPU:6, one launch (start us, length us, event | category | flops | bytes accessed | tf_op | source)
XLA Modules:
  0.0 56.3 jit_solution(15992380332805185736)
XLA Ops:
  0.0 0.7 %pad_add_fusion.table_hbm = s32[128]{0:T(128)S(1)} fusion(s32[64]{0:T(128)} %param.5, s32[64]{0:T(128)} %param.4), kind=kLoop, calls=%fused_computation | loop fusion | flops 128 | bytes 1024 | tf_op jit(solution)/shard_map/concatenate | solution.py:364
  0.7 0.0 copy-start
  0.7 1.1 %copy-done = f32[1,64,2400]{2,1,0:T(8,128)S(1)} copy-done((f32[1,64,2400]{2,1,0:T(8,128)S(1)}, f32[1,64,2400]{2,1,0:T(8,128)}, u32[]{:S(2)}) %copy-start) | copy-done | bytes 614424
  1.8 53.6 %correlate.1 = f32[3,61,8,64]{3,2,1,0:T(8,128)S(1)} custom-call(s32[128]{0:T(128)S(1)} %pad_add_fusion.table_hbm, f32[1,64,2400]{2,1,0:T(8,128)S(1)} %copy-done), custom_call_target="tpu_custom_call" | custom-call | flops 3825205248 | bytes 1048576 | tf_op jit(solution)/shard_map/correlate/pallas_call | solution.py:337
  55.5 0.9 %copy.5 = f32[3,8,61,64]{3,1,2,0:T(8,128)} copy(f32[3,8,61,64]{3,1,2,0:T(8,128)S(1)} %bitcast.1) | data formatting | bytes 749568
Async XLA Ops:
  0.7 1.1 %copy-start = (f32[1,64,2400]{2,1,0:T(8,128)S(1)}, f32[1,64,2400]{2,1,0:T(8,128)}, u32[]{:S(2)}) copy-start(f32[1,64,2400]{2,1,0:T(8,128)} %x_hbm.1) | copy-start | bytes 1843204

commit v9 on v8

--- a/solution.py
+++ b/solution.py
@@ -31,9 +31,9 @@
 BF16 = jnp.bfloat16
 
 
-def kernel(table_hbm, x_hbm, out_hbm, table, x_ref, wide, gathered, first, far, full,
-           shifted, acc, outgoing, incoming, result, load, first_s, first_r, own_s, own_r, far_s, far_r, full_r,
-           line_s, core_s, core_r, sum_s, sum_r, out_s, token):
+def kernel(table_hbm, x_hbm, out_ref, table, x_ref, wide, gathered, first, far, full,
+           shifted, acc, outgoing, incoming, load, first_s, first_r, own_s, own_r, far_s, far_r, full_r,
+           line_s, core_s, core_r, sum_s, sum_r, token):
     b = lax.axis_index("block")
     d = lax.axis_index("day")
     z = b // PLANE
@@ -249,30 +249,19 @@
             outgoing.at[s], incoming.at[s], sum_s.at[s], sum_r.at[s],
             device_id=at_device(0, p, x * 2 + 1 - yh), device_id_type=MESH)
 
-    def out_copy(s):
-        return pltpu.make_async_copy(result.at[s, pl.ds(0, LAGS)], out_hbm.at[s], out_s.at[s])
-
-    def half_rows(s, n, half):
-        return acc[s, pl.ds(pl.multiple_of(16 * n + 8 * half, 8), 8), :]
+    def halves(s):
+        whole = acc[s].reshape(OWNER_SHIFTS, 2, SHARE // 2, COLS)
+        return whole[:, 0].reshape(ROWS, COLS), whole[:, 1].reshape(ROWS, COLS)
 
     def to_partner(s):
-        def pair(n):
-            rows = jnp.concatenate([half_rows(s, 2 * n, 1 - yh), half_rows(s, 2 * n + 1, 1 - yh)], axis=0)
-            outgoing[s, pl.ds(pl.multiple_of(16 * n, 16), 16), :] = rows.astype(BF16)
-        each(0, OWNER_SHIFTS // 2, pair)
+        top, low = halves(s)
+        outgoing[s] = jnp.where(yh == 0, low, top).astype(BF16)
         sum_copy(s).start()
 
     def finish(s):
         sum_copy(s).wait_recv()
-
-        def pair(n):
-            got = incoming[s, pl.ds(pl.multiple_of(16 * n, 16), 16), :].astype(F32)
-            for k in range(2):
-                sums = (half_rows(s, 2 * n + k, yh) + got[8 * k:8 * k + 8]) * (float(DAYS * SEG) ** -0.5)
-                for r in range(OWN_SHIFTS):
-                    result[s, OWN_SHIFTS * (2 * n + k) + r] = sums[:, CAP * r:CAP * r + CAP]
-        each(0, OWNER_SHIFTS // 2, pair)
-        out_copy(s).start()
+        top, low = halves(s)
+        out_ref[s] = (jnp.where(yh == 0, top, low) + incoming[s].astype(F32)) * (float(DAYS * SEG) ** -0.5)
 
     each(0, STEPS, open_owner)
     each(1, NX, own_shifts)
@@ -326,7 +315,6 @@
 
     def done(s):
         sum_copy(s).wait_send()
-        out_copy(s).wait()
 
     each(0, STEPS, done)
 
@@ -336,9 +324,9 @@
     tile = (16, 128)
     raw = pl.pallas_call(
         kernel,
-        out_shape=jax.ShapeDtypeStruct((STEPS, LAGS, SHARE // 2, CAP), F32),
+        out_shape=jax.ShapeDtypeStruct((STEPS, ROWS, COLS), F32),
         in_specs=[pl.BlockSpec(memory_space=pltpu.HBM)] * 2,
-        out_specs=pl.BlockSpec(memory_space=pltpu.HBM),
+        out_specs=pl.BlockSpec(memory_space=pltpu.VMEM),
         scratch_shapes=[
             pltpu.SMEM((2 * N_BLOCK,), jnp.int32),
             pltpu.VMEM((NX, 16, SEG), F32),
@@ -351,18 +339,19 @@
             pltpu.VMEM((STEPS, 2 * ROWS, COLS), F32),
             pltpu.VMEM((STEPS, ROWS, COLS), BF16),
             pltpu.VMEM((STEPS, ROWS, COLS), BF16),
-            pltpu.VMEM((STEPS, OWN_SHIFTS * OWNER_SHIFTS, SHARE // 2, CAP), F32),
             dma((NX + 1,)), dma((CLASSES * NX,)), dma((CLASSES * PLANE,)), dma((NX,)), dma((NX,)),
             dma((STEPS, CLASSES)), dma((STEPS, CLASSES)), dma((STEPS * PLANE, CLASSES)),
-            dma((STEPS, 7)), dma((STEPS, PLANE)), dma((STEPS, PLANE)), dma((STEPS,)), dma((STEPS,)), dma((STEPS,)),
+            dma((STEPS, 7)), dma((STEPS, PLANE)), dma((STEPS, PLANE)), dma((STEPS,)), dma((STEPS,)),
             pltpu.SemaphoreType.REGULAR,
         ],
         compiler_params=pltpu.CompilerParams(
-            collective_id=0, has_side_effects=True, vmem_limit_bytes=48 << 20),
+            collective_id=0, has_side_effects=True, vmem_limit_bytes=54800 << 10),
         cost_estimate=pl.CostEstimate(flops=2 * STEPS * ROWS * COLS * K * DAYS, bytes_accessed=1 << 20, transcendentals=0),
         name="correlate",
     )(jnp.concatenate([counts, order]), traces)
-    return raw.transpose(0, 2, 1, 3)
+    parts = raw.reshape(STEPS, OWNER_SHIFTS, SHARE // 2, OWN_SHIFTS, CAP)
+    lags = parts.transpose(0, 2, 1, 3, 4).reshape(STEPS, SHARE // 2, OWNER_SHIFTS * OWN_SHIFTS, CAP)
+    return lags[:, :, :LAGS]
 
 
 def solution(mesh):

time: 57.3 us -> 54.9 us (0.958); the launches traced: 56.3 us -> 54.8 us
  Pallas kernels: 53.6 us -> 52.7 us
  local copies, waits for them, and re-layouts: 1.95 us -> 1.31 us
    unnamed x3 -> x0, local copies, waits for them, and re-layouts: 1.95 us -> none
    pallas_call x1, Pallas kernels: 53.6 us -> 52.7 us  [per_device(): pl.pallas_call(kernel, out_shape=jax.ShapeDtypeStruct((STEPS, ROWS, COLS)...]
    slice x0 -> x1, local copies, waits for them, and re-layouts: none -> 0.92 us  [per_device(): return lags[:, :, :LAGS]]
where the time goes in v9:
time: 54.9 us; the launch traced here: 54.8 us
  Pallas kernels  52.7 us (96%)
  local copies, waits for them, and re-layouts  1.31 us (2%)
  other arithmetic  0.75 us (1%)
    pallas_call x1, Pallas kernels, per_device(): pl.pallas_call(kernel, out_shape=jax.ShapeDtypeStruct((STEPS, ROWS, COLS)...  52.7 us

profile of v9, /device:TPU:6, one launch (start us, length us, event | category | flops | bytes accessed | tf_op | source)
XLA Modules:
  0.0 54.8 jit_solution(12725868933202444064)
XLA Ops:
  0.0 0.7 %pad_add_fusion.table_hbm = s32[128]{0:T(128)S(1)} fusion(s32[64]{0:T(128)} %param.5, s32[64]{0:T(128)} %param.4), kind=kLoop, calls=%fused_computation | loop fusion | flops 128 | bytes 1024 | tf_op jit(solution)/shard_map/concatenate | solution.py:351
  0.7 52.7 %correlate.1 = f32[3,128,256]{2,1,0:T(8,128)S(1)} custom-call(s32[128]{0:T(128)S(1)} %pad_add_fusion.table_hbm, f32[1,64,2400]{2,1,0:T(8,128)} %x_hbm.1), custom_call_target="tpu_custom_call" | custom-call | flops 3825205248 | bytes 1048576 | tf_op jit(solution)/shard_map/correlate/pallas_call | solution.py:325
  53.5 0.3 reshape.6
  53.8 0.1 copy.4
  53.9 0.9 %slice.4 = f32[3,8,61,64]{3,1,2,0:T(8,128)} slice(f32[3,8,64,64]{3,1,2,0:T(8,128)S(1)} %bitcast.3), slice={[0:3], [0:8], [0:61], [0:64]} | slice | bytes 749568 | tf_op jit(solution)/shard_map/slice | solution.py:354
